TPU v7x, 512 devices: a whole 4x8x8 slice. The times are simulated.
512 devices in a mesh: blk: 128 (over x, z, y_hi, core), rep: 4 (over y_lo).
Axes of the slice: x: 4, y: 8 (y_hi: 2, y_lo: 4; y = y_hi * 4 + y_lo), z: 8, core: 2. Of those that a mesh axis runs over, the one named last changes fastest.
Arguments:
- texts: bfloat16 [2048, 512], P(('blk', 'rep')), may hold values from -5 to 5
- frames: bfloat16 [2048, 48, 512], P('blk'), may hold values from -30 to 30
- frame_mask: int32 [2048, 48], P('blk'), may hold values from 0 to 1, as said below
- cotangent: float32 [2048, 2048], P(None, 'blk'), may hold values from -24 to 24
Outputs:
- text_grad: bfloat16 [2048, 512], P(('blk', 'rep'))
- frame_grad: bfloat16 [2048, 48, 512], P(('blk', 'rep'))
Inputs may be any that keep to these rules, and one draw needn't show every extreme that they name: `frame_mask`: each clip's real frames are its first n frames, 4 <= n <= 48; some clip has all 48.
All inputs are finite; a program needn't handle non-finite values.
Results may differ from a plain program's by a relative error of at most 0.015.
Values may be sent and summed in bfloat16 or wider, within the bound.
A program may use at most 64 MiB of HBM per device.

v0:
```python
from functools import partial
import math

import jax
import jax.numpy as jnp
from jax import lax
from jax.sharding import PartitionSpec as P

EPSILON = 1e-05


def pair_block(frame_acc, inputs, frames, live_mask, factor):
    text_rows, cot_rows = inputs
    scores = (
        jnp.einsum("td,cfd->tcf", text_rows, frames, preferred_element_type=jnp.float32) * factor
    )
    scores = jnp.where(live_mask[None], scores, -1e30)
    highest = jnp.max(scores, axis=2, keepdims=True)
    raw_weights = jnp.exp(scores - highest)
    probs = raw_weights / jnp.sum(raw_weights, axis=2, keepdims=True)
    probs_low = probs.astype(jnp.bfloat16)
    pooled = jnp.einsum("tcf,cfd->tcd", probs_low, frames, preferred_element_type=jnp.float32)
    inverse = lax.rsqrt(jnp.mean(pooled * pooled, axis=2, keepdims=True) + EPSILON)
    normed = pooled * inverse
    text_part = jnp.sum(cot_rows[:, :, None] * normed, axis=1) * factor
    upstream = cot_rows[:, :, None] * text_rows.astype(jnp.float32)[:, None, :] * factor
    projected = jnp.mean(upstream * normed, axis=2, keepdims=True)
    pooled_grad = inverse * (upstream - normed * projected)
    pooled_low = pooled_grad.astype(jnp.bfloat16)
    prob_grad = jnp.einsum("tcd,cfd->tcf", pooled_low, frames, preferred_element_type=jnp.float32)
    centred = jnp.sum(probs * prob_grad, axis=2, keepdims=True)
    score_grad = probs * (prob_grad - centred)
    score_low = score_grad.astype(jnp.bfloat16)
    frame_term = jnp.einsum(
        "tcf,tcd->cfd", probs_low, pooled_low, preferred_element_type=jnp.float32
    )
    frame_term = frame_term + factor * jnp.einsum(
        "tcf,td->cfd", score_low, text_rows, preferred_element_type=jnp.float32
    )
    text_term = text_part + factor * jnp.einsum(
        "tcf,cfd->td", score_low, frames, preferred_element_type=jnp.float32
    )
    return (frame_acc + frame_term, text_term)


def grads_dense(text_rows, cot_rows, frames, live_mask, factor):
    total_rows = text_rows.shape[0]
    block_rows = math.gcd(total_rows, 64)
    count_blocks = total_rows // block_rows
    feature_dim = text_rows.shape[1]
    clips_here = frames.shape[0]
    stacked = (
        text_rows.reshape(count_blocks, block_rows, feature_dim),
        cot_rows.reshape(count_blocks, block_rows, clips_here),
    )
    zero_grads = jnp.zeros(frames.shape, jnp.float32)
    stepper = partial(pair_block, frames=frames, live_mask=live_mask, factor=factor)
    frame_total, text_blocks = lax.scan(stepper, zero_grads, stacked)
    return (text_blocks.reshape(total_rows, feature_dim), frame_total)


def pair_grads(text_rows, cot_rows, frames, live_mask, factor):
    return grads_dense(text_rows, cot_rows, frames, live_mask, factor)


def per_device(texts, frames, frame_mask, cotangent):
    feature_dim = frames.shape[2]
    factor = 1.0 / math.sqrt(feature_dim)
    rep_size = lax.axis_size("rep")
    blk_size = lax.axis_size("blk")
    rep_index = lax.axis_index("rep")
    text_dev = texts.shape[0]
    clips_here = frames.shape[0]
    group_cot = cotangent.reshape(blk_size, rep_size, text_dev, clips_here)
    group_cot = lax.dynamic_index_in_dim(group_cot, rep_index, 1, keepdims=False)
    group_cot = group_cot.reshape(blk_size * text_dev, clips_here)
    live_mask = frame_mask > 0
    gathered = lax.all_gather(texts, "blk", axis=0, tiled=True)
    text_part, frame_part = pair_grads(gathered, group_cot, frames, live_mask, factor)
    text_out = lax.psum_scatter(text_part, "blk", scatter_dimension=0, tiled=True).astype(
        jnp.bfloat16
    )
    frame_out = lax.psum_scatter(
        frame_part.astype(jnp.bfloat16), "rep", scatter_dimension=0, tiled=True
    )
    return (text_out, frame_out)


def solution(mesh):
    return jax.shard_map(
        per_device,
        mesh=mesh,
        in_specs=(P(("blk", "rep"), None), P("blk", None, None), P("blk", None), P(None, "blk")),
        out_specs=(P(("blk", "rep"), None), P(("blk", "rep"), None, None)),
        check_vma=False,
    )
```

profile of v0, /device:TPU:1, one launch (start us, length us, event | category | flops | bytes accessed | tf_op | source)
XLA Modules:
  0.0 1148.8 jit_solution(1748456281152766686)
XLA Ops:
  7.3 1.3 copy.8
  8.7 233.4 %all-gather = bf16[128,4,512]{2,1,0:T(4,128)(2,1)S(1)} all-gather(bf16[1,4,512]{2,1,0:T(4,128)(2,1)} %bitcast.95), channel_id=1, replica_groups=mesh['blk'=128,'rep'=4] {'blk'}, dimensions={0}, use_global_device_ids=true | all-gather | bytes 528384 | tf_op jit(solution)/shard_map/all_gather | solution.py:78
  242.1 0.9 reshape.37
  243.1 99.3 %while.13 = (s32[]{:T(128)}, f32[16,48,512]{2,1,0:T(8,128)}, f32[8,64,512]{2,1,0:T(8,128)}, pred[16,48]{1,0:T(8,128)(4,1)S(1)}, bf16[8,64,512]{2,1,0:T(8,128)(2,...) while((s32[]{:T(128)}, f32[16,48,512]{2,1,0:T(8,128)}, ...), condition=%wide.region_7.8_spmd.clone, body=%wide.region_0.7_spmd.clone.sunk | while | flops 316524672 | bytes 21887372 | solution.py:58
  243.1 1.2 fusion.58
  244.3 0.8 fusion.59
  245.7 0.9 bitcast_convert_fusion.2
  246.6 0.7 multiply_reduce_fusion.5
  247.3 0.9 multiply_reduce_fusion.6
  248.3 0.9 fusion.62
  249.2 2.3 fusion.61
  251.6 3.5 select_add_fusion.2
  255.1 1.2 fusion.58
  256.3 0.8 fusion.59
  257.7 0.9 bitcast_convert_fusion.2
  259.3 0.9 multiply_reduce_fusion.6
  260.3 0.9 fusion.62
  261.2 2.3 fusion.61
  263.6 4.0 select_add_fusion.2
  267.5 1.2 fusion.58
  268.7 0.8 fusion.59
  270.2 0.9 bitcast_convert_fusion.2
  271.8 0.9 multiply_reduce_fusion.6
  272.8 1.0 fusion.62
  273.7 2.3 fusion.61
  276.1 4.0 select_add_fusion.2
  280.0 1.2 fusion.58
  281.2 0.8 fusion.59
  282.7 0.9 bitcast_convert_fusion.2
  284.3 0.9 multiply_reduce_fusion.6
  285.3 0.9 fusion.62
  286.2 2.3 fusion.61
  288.5 4.0 select_add_fusion.2
  292.5 1.2 fusion.58
  293.7 0.8 fusion.59
  295.1 0.9 bitcast_convert_fusion.2
  296.8 0.9 multiply_reduce_fusion.6
  297.7 0.9 fusion.62
  298.6 2.3 fusion.61
  301.0 4.0 select_add_fusion.2
  304.9 1.2 fusion.58
  306.1 0.8 fusion.59
  307.6 0.9 bitcast_convert_fusion.2
  309.2 0.9 multiply_reduce_fusion.6
  310.2 0.9 fusion.62
  311.1 2.3 fusion.61
  313.4 4.0 select_add_fusion.2
  317.4 1.2 fusion.58
  318.6 0.8 fusion.59
  320.1 0.9 bitcast_convert_fusion.2
  321.7 0.9 multiply_reduce_fusion.6
  322.6 0.9 fusion.62
  323.6 2.3 fusion.61
  325.9 4.0 select_add_fusion.2
  329.9 1.2 fusion.58
  331.1 0.8 fusion.59
  332.5 0.9 bitcast_convert_fusion.2
  334.1 0.9 multiply_reduce_fusion.6
  335.1 1.0 fusion.62
  336.1 2.3 fusion.61
  338.4 4.0 select_add_fusion.2
  342.4 2.5 convert_element_type.23
  344.9 1.3 dynamic-slice
  346.8 794.5 %all-reduce.2 = bf16[512,512]{1,0:T(8,128)(2,1)S(1)} all-reduce(f32[512,512]{1,0:T(8,128)S(1)} %bitcast.94), channel_id=2, replica_groups=mesh['blk'=128,'rep'=4] {'blk'}, use_global_device_ids=true, to_apply=%region_8.9.clone | all-reduce | flops 262144 | bytes 1572864
  (78 shorter events, 10.9 us)
Async XLA Ops:
  7.2 235.9 %copy-start.3 = (s32[16,48]{1,0:T(8,128)S(1)}, s32[16,48]{1,0:T(8,128)}, u32[]{:S(2)}) copy-start(s32[16,48]{1,0:T(8,128)} %param.8) | copy-start | bytes 9220
  7.2 235.9 %copy-start = (bf16[16,48,512]{2,1,0:T(8,128)(2,1)S(1)}, bf16[16,48,512]{2,1,0:T(8,128)(2,1)}, u32[]{:S(2)}) copy-start(bf16[16,48,512]{2,1,0:T(8,128)(2,1)} %param.7) | copy-start | bytes 2359300
  7.2 1134.7 %reduce-scatter.2.cloned.1.call-start = ((), (), s32[]{:S(2)}) async-start(), calls=%async_computation.1 | async-start | bytes 983040 | tf_op jit(solution)/shard_map/reduce_scatter | solution.py:83
  245.7 1.6 copy-start.1
  257.7 1.6 copy-start.1
  270.2 1.6 copy-start.1
  282.6 1.6 copy-start.1
  295.1 1.6 copy-start.1
  307.6 1.6 copy-start.1
  320.0 1.6 copy-start.1
  332.5 1.6 copy-start.1
  342.4 4.5 copy-start.2
Sparse Core Ops, SparseCore 0:
  345.0 19.3 reduce-scatter.1
where the time goes:
time: 1160 us; the launch traced here: 1150 us
  blocking collectives  1030 us (89%)
  matrix products  78.6 us (7%)
  other arithmetic  22.5 us (2%)
  between operations  14.7 us (1%)
    unnamed x1, blocking collectives  794 us
    all_gather x1, blocking collectives, per_device(): gathered = lax.all_gather(texts, 'blk', axis=0, tiled=True)  233 us
    dot_general x8, matrix products, pair_block(): jnp.einsum('tcf,tcd->cfd', probs_low, pooled_low, preferred_element_type=...  31.3 us
  transfers between devices with their start and end apart: 1, of which 0 were waited for; matrix products, arithmetic and copies ran while one was open for 0% of the time, Pallas kernels for 0%

commit v1 on v0

v1 whole, which is shorter than its diff:
```python
import math

import jax
import jax.numpy as jnp
from jax import lax
from jax.experimental import pallas as pl
from jax.experimental.pallas import tpu as pltpu
from jax.sharding import PartitionSpec as P

MESH = pl.DeviceIdType.MESH
EPSILON = 1e-05
NX, NZ, NY = 4, 8, 8
D, FR, C_DEV, ROWS = 512, 48, 16, 4
CHUNK = 128
GROUP = 192
ORDER = (0, 1, 3, 2)
FACTOR = 1.0 / math.sqrt(D)
F32, BF16 = jnp.float32, jnp.bfloat16


def dot(a, b, ca, cb):
    return lax.dot_general(a, b, (((ca,), (cb,)), ((), ())), preferred_element_type=F32)


def swap(v):
    return pltpu.roll(v, 4, axis=1)


def tiles_to_rows(tiles):
    n = tiles.shape[0]
    pairs = tiles.reshape(n // 2, 2, 16, 128)
    low = lax.broadcasted_iota(jnp.int32, (n // 2, 8, 128), 1) < 4
    out = []
    for half in range(2):
        a = pairs[:, 0, 8 * half : 8 * half + 8]
        b = pairs[:, 1, 8 * half : 8 * half + 8]
        out.append(jnp.where(low, a, swap(b)).reshape(4 * n, 128))
        out.append(jnp.where(low, swap(a), b).reshape(4 * n, 128))
    return out


def rows_to_tiles(rows):
    n = rows.shape[0] // 4
    low = lax.broadcasted_iota(jnp.int32, (n // 2, 8, 128), 1) < 4
    blocks = [rows[:, 128 * k : 128 * k + 128].reshape(n // 2, 8, 128) for k in range(4)]
    first, second = [], []
    for half in range(2):
        a, b = blocks[2 * half], blocks[2 * half + 1]
        first.append(jnp.where(low, a, swap(b)))
        second.append(jnp.where(low, swap(a), b))
    first = jnp.concatenate(first, axis=1)
    second = jnp.concatenate(second, axis=1)
    return jnp.stack([first, second], axis=1).reshape(n, 16, 128)


def kernel(
    texts_ref, frames_ref, mask_ref, cot_ref, text_out, frame_out,
    frames, cot, z_texts, texts_in, texts, cot_sel, counts, gram_hi, gram_lo,
    probs_low, weights, scaled, text_tiles, core_send, core_recv, xy_send, xy_recv,
    z_send, z_recv, frame_send, frame_recv,
    load_sem, ag_z_send, ag_z_recv, ag_xy_send, ag_xy_recv, ag_c_send, ag_c_recv,
    rs_c_send, rs_c_recv, rs_xy_send, rs_xy_recv, rs_z_send, rs_z_recv, fr_send, fr_recv,
):
    blk, rep = lax.axis_index("blk"), lax.axis_index("rep")
    core = blk % 2
    y = (blk // 2) % 2 * 4 + rep
    z = blk // 4 % NZ
    x = blk // 32
    odd, half = y % 2, y // 2
    parity = half % 2
    handlers = ((2 * half + 1 - parity) % NY, (2 * half + NY - 1 + 3 * parity) % NY)
    pair = (half + parity + odd + 3) % 4
    slot = (half + 1 - odd) % 2
    own = slot == 0

    def device(xx, zz, yy, cc):
        return (((xx * NZ + zz) * 2 + yy // 4) * 2 + cc, yy % 4)

    sibling = device(x, z, y, 1 - core)

    def send(src, dst, send_sem, recv_sem, to):
        return pltpu.make_async_remote_copy(
            src_ref=src, dst_ref=dst, send_sem=send_sem, recv_sem=recv_sem, device_id=to, device_id_type=MESH
        )

    def arrived(ref, sem):
        pltpu.make_async_copy(ref, ref, sem).wait()

    loads = [pltpu.make_async_copy(cot_ref, cot, load_sem.at[4])]
    for g in range(4):
        loads.append(pltpu.make_async_copy(frames_ref.at[pl.ds(4 * g, 4)], frames.at[pl.ds(4 * g, 4)], load_sem.at[g]))
    for load in loads:
        load.start()

    barrier = pltpu.get_barrier_semaphore()

    def greet(to):
        pl.semaphore_signal(barrier, inc=1, device_id=to, device_id_type=MESH)

    greet(sibling)
    for dz in range(1, NZ):
        greet(device(x, (z + dz) % NZ, y, core))
    for k in range(1, 4):
        greet((blk, (rep + k) % 4))
    for dx in range(NX):
        xx = (x + dx) % NX
        for h in range(2):
            if dx == 0 and h == 0:

                @pl.when(jnp.logical_not(own))
                def _():
                    greet(device(x, z, handlers[0], core))
                    greet(device(x, z, 2 * pair + odd, core))

                greet(device(x, z, 2 * pair + 1 - odd, core))
            else:
                greet(device(xx, z, handlers[h], core))
                if dx > 0:
                    greet(device(xx, z, 2 * pair + h, core))

    rows = texts_ref[...].astype(F32)
    tile = jnp.concatenate([rows[:, 128 * k : 128 * k + 128] for k in range(4)], axis=0)
    z_texts[z] = tile.astype(BF16)

    @pl.when(own)
    def _():
        pl.semaphore_wait(barrier, 1 + 7 + 3 + 16 - 2)

    @pl.when(jnp.logical_not(own))
    def _():
        pl.semaphore_wait(barrier, 1 + 7 + 3 + 16)

    for dz in range(1, NZ):
        to = (z + dz) % NZ
        send(z_texts.at[z], z_texts.at[z], ag_z_send.at[dz], ag_z_recv.at[z], device(x, to, y, core)).start()

    pltpu.make_async_copy(cot_ref, cot, load_sem.at[4]).wait()
    picked = lax.broadcasted_iota(jnp.int32, (512, CHUNK), 0)
    lane = lax.broadcasted_iota(jnp.int32, (512, CHUNK), 1)
    wanted = (
        lane % 32 // 4 * 64 + pair // 2 * 32 + lane // 64 * 16 + pair % 2 * 8 + lane // 32 % 2 * 4 + lane % 4
    )
    choose = jnp.where(picked == wanted, 1.0, 0.0).astype(BF16)
    for xx in range(NX):
        wide = cot[:, 512 * xx : 512 * xx + 512]
        high = wide.astype(BF16)
        low = (wide - high.astype(F32)).astype(BF16)
        cot_sel[xx] = dot(high, choose, 1, 0) + dot(low, choose, 1, 0)
    totals = jnp.sum(mask_ref[...].astype(F32), axis=1, keepdims=True)
    counts[...] = jnp.broadcast_to(totals, (C_DEV, CHUNK))
    same = (
        lax.broadcasted_iota(jnp.int32, (GROUP, GROUP), 0) // FR
        == lax.broadcasted_iota(jnp.int32, (GROUP, GROUP), 1) // FR
    )

    def group_frames(g):
        return frames[4 * g : 4 * g + 4].reshape(GROUP, D)

    for g in range(4):
        loads[1 + g].wait()
        block = group_frames(g)
        gram = jnp.where(same, dot(block, block, 1, 1), 0.0)
        high = gram.astype(BF16)
        gram_hi[g] = high
        gram_lo[g] = (gram - high.astype(F32)).astype(BF16)

    for dz in range(1, NZ):
        source = (z + dz) % NZ
        arrived(z_texts.at[source], ag_z_recv.at[source])

    def to_handler(dx, h):
        xx = (x + dx) % NX
        return send(
            z_texts, texts_in.at[x, core, odd], ag_xy_send.at[dx, h], ag_xy_recv.at[x, odd],
            device(xx, z, handlers[h], core),
        )

    for dx in (2, 1, 3, 0):
        for h in range(2):
            if dx == 0 and h == 0:

                @pl.when(own)
                def _():
                    pltpu.make_async_copy(z_texts, texts_in.at[x, core, odd], ag_xy_recv.at[x, odd]).start()

                @pl.when(jnp.logical_not(own))
                def _():
                    to_handler(0, 0).start()
            else:
                to_handler(dx, h).start()

    def share(i):
        xx = (x + ORDER[i]) % NX
        for rr in range(2):
            arrived(texts_in.at[xx, core, rr], ag_xy_recv.at[xx, rr])
        send(texts_in.at[xx, core], texts_in.at[xx, core], ag_c_send.at[i], ag_c_recv.at[i], sibling).start()

    def work(i):
        xx = (x + ORDER[i]) % NX
        arrived(texts_in.at[xx, 1 - core], ag_c_recv.at[i])
        columns = slice(CHUNK * i, CHUNK * i + CHUNK)
        tiles = texts_in[xx].reshape(32, 16, 128).astype(F32)
        for k, block in enumerate(tiles_to_rows(tiles)):
            texts[columns, 128 * k : 128 * k + 128] = block.astype(BF16)
        chunk = texts[columns, :]
        cot_rows = cot_sel[xx]
        frame_index = lax.broadcasted_iota(jnp.int32, (FR, CHUNK), 0).astype(F32)
        for g in range(4):
            scores = dot(group_frames(g), chunk, 1, 1)
            kept = []
            for q in range(4):
                raw = scores[FR * q : FR * q + FR]
                live = frame_index < counts[4 * g + q : 4 * g + q + 1, :]
                masked = jnp.where(live, raw * FACTOR, -1e30)
                top = jnp.max(masked, axis=0, keepdims=True)
                grown = jnp.exp(masked - top)
                probs = grown * (1.0 / jnp.sum(grown, axis=0, keepdims=True))
                low = probs.astype(BF16)
                kept.append((raw, probs, low))
            group_low = jnp.concatenate([low for _, _, low in kept], axis=0)
            rows = slice(GROUP * g, GROUP * g + GROUP)
            probs_low[rows, columns] = group_low
            against = dot(gram_hi[g], group_low, 1, 0) + dot(gram_lo[g], group_low, 1, 0)
            for q in range(4):
                raw, probs, low = kept[q]
                low = low.astype(F32)
                with_pooled = against[FR * q : FR * q + FR]
                square = jnp.maximum(jnp.sum(low * with_pooled, axis=0, keepdims=True), 0.0)
                inner = jnp.sum(low * raw, axis=0, keepdims=True)
                inverse = lax.rsqrt(square * (1.0 / D) + EPSILON)
                up = inverse * cot_rows[4 * g + q : 4 * g + q + 1, :] * FACTOR
                back = up * inverse * inverse * inner * (1.0 / D)
                prob_grad = up * raw - back * with_pooled
                centred = jnp.sum(probs * prob_grad, axis=0, keepdims=True)
                score_grad = probs * (prob_grad - centred)
                at = slice(GROUP * g + FR * q, GROUP * g + FR * q + FR)
                weights[at, columns] = (up * low + FACTOR * score_grad).astype(BF16)
                scaled[at, columns] = (back * low).astype(BF16)
        part = dot(weights[:, columns], frames[...].reshape(C_DEV * FR, D), 0, 0)
        text_tiles[i] = rows_to_tiles(part).reshape(2, 16, 16, 128)
        core_send[i] = text_tiles[i, 1 - core].astype(BF16)
        send(core_send.at[i], core_recv.at[i], rs_c_send.at[i], rs_c_recv.at[i], sibling).start()

    def text_home(i, rr):
        xx = (x + ORDER[i]) % NX
        return send(
            xy_send.at[i, rr], xy_recv.at[x, slot], rs_xy_send.at[i, rr], rs_xy_recv.at[x, slot],
            device(xx, z, 2 * pair + rr, core),
        )

    def combine(i):
        arrived(core_recv.at[i], rs_c_recv.at[i])
        both = text_tiles[i, core] + core_recv[i].astype(F32)
        xy_send[i] = both.astype(BF16).reshape(2, NZ, 16, 128)
        for rr in range(2):
            if i == 0:
                stays = jnp.logical_and(own, odd == rr)

                @pl.when(stays)
                def _():
                    pltpu.make_async_copy(xy_send.at[0, rr], xy_recv.at[x, slot], rs_xy_recv.at[x, slot]).start()

                @pl.when(jnp.logical_not(stays))
                def _():
                    text_home(0, rr).start()
            else:
                text_home(i, rr).start()

    share(0)
    share(1)
    work(0)
    share(2)
    work(1)
    combine(0)
    share(3)
    work(2)
    combine(1)
    work(3)
    combine(2)

    def frame_home(g):
        return send(frame_send.at[g], frame_recv.at[rep], fr_send.at[g], fr_recv.at[rep], (blk, g))

    for g in range(4):
        rows = slice(GROUP * g, GROUP * g + GROUP)
        mixed = jnp.where(same, dot(scaled[rows, :], probs_low[rows, :], 1, 1), 0.0)
        grad = dot(weights[rows, :], texts[...], 1, 0) - dot(mixed.astype(BF16), group_frames(g), 1, 0)
        frame_send[g] = grad.astype(BF16)

        @pl.when(rep != g)
        def _():
            frame_home(g).start()

        if g == 0:
            combine(3)

    for h in range(2):
        for dx in ORDER:
            xx = (x + dx) % NX
            arrived(xy_recv.at[xx, h], rs_xy_recv.at[xx, h])
    z_send[...] = jnp.sum(xy_recv[...].reshape(8, NZ, 16, 128).astype(F32), axis=0).astype(BF16)
    for dz in range(1, NZ):
        to = (z + dz) % NZ
        send(z_send.at[to], z_recv.at[z], rs_z_send.at[dz], rs_z_recv.at[z], device(x, to, y, core)).start()
    z_recv[z] = z_send[z]

    total = frame_send[rep].astype(F32)
    for k in range(1, 4):
        source = (rep + k) % 4
        arrived(frame_recv.at[source], fr_recv.at[source])
        total = total + frame_recv[source].astype(F32)
    frame_out[...] = total.astype(BF16).reshape(4, FR, D)

    for dz in range(1, NZ):
        source = (z + dz) % NZ
        arrived(z_recv.at[source], rs_z_recv.at[source])
    tile = jnp.sum(z_recv[...].astype(F32), axis=0)
    text_out[...] = jnp.concatenate([tile[4 * k : 4 * k + 4] for k in range(4)], axis=1).astype(BF16)

    for dz in range(1, NZ):
        to = (z + dz) % NZ
        send(z_texts.at[z], z_texts.at[z], ag_z_send.at[dz], ag_z_recv.at[z], device(x, to, y, core)).wait_send()
        send(z_send.at[to], z_recv.at[z], rs_z_send.at[dz], rs_z_recv.at[z], device(x, to, y, core)).wait_send()
    for dx in range(NX):
        for h in range(2):
            if dx == 0 and h == 0:

                @pl.when(jnp.logical_not(own))
                def _():
                    to_handler(0, 0).wait_send()
            else:
                to_handler(dx, h).wait_send()
    for i in range(4):
        xx = (x + ORDER[i]) % NX
        send(texts_in.at[xx, core], texts_in.at[xx, core], ag_c_send.at[i], ag_c_recv.at[i], sibling).wait_send()
        send(core_send.at[i], core_recv.at[i], rs_c_send.at[i], rs_c_recv.at[i], sibling).wait_send()
        for rr in range(2):
            if i == 0:

                @pl.when(jnp.logical_not(jnp.logical_and(own, odd == rr)))
                def _():
                    text_home(0, rr).wait_send()
            else:
                text_home(i, rr).wait_send()
    for g in range(4):

        @pl.when(rep != g)
        def _():
            frame_home(g).wait_send()


def per_device(texts, frames, frame_mask, cotangent):
    vmem, dma = pltpu.VMEM, pltpu.SemaphoreType.DMA
    whole = pl.BlockSpec(memory_space=pltpu.VMEM)
    remote = pl.BlockSpec(memory_space=pl.ANY)
    clip_rows = C_DEV * FR
    return pl.pallas_call(
        kernel,
        out_shape=(
            jax.ShapeDtypeStruct((ROWS, D), BF16),
            jax.ShapeDtypeStruct((4, FR, D), BF16),
        ),
        in_specs=[whole, remote, whole, remote],
        out_specs=(whole, whole),
        scratch_shapes=[
            vmem((C_DEV, FR, D), BF16),
            vmem((C_DEV, 2048), F32),
            vmem((NZ, 16, 128), BF16),
            vmem((NX, 2, 2, NZ, 16, 128), BF16),
            vmem((4 * CHUNK, D), BF16),
            vmem((NX, C_DEV, CHUNK), F32),
            vmem((C_DEV, CHUNK), F32),
            vmem((4, GROUP, GROUP), BF16),
            vmem((4, GROUP, GROUP), BF16),
            vmem((clip_rows, 4 * CHUNK), BF16),
            vmem((clip_rows, 4 * CHUNK), BF16),
            vmem((clip_rows, 4 * CHUNK), BF16),
            vmem((4, 2, 16, 16, 128), F32),
            vmem((4, 16, 16, 128), BF16),
            vmem((4, 16, 16, 128), BF16),
            vmem((4, 2, NZ, 16, 128), BF16),
            vmem((NX, 2, NZ, 16, 128), BF16),
            vmem((NZ, 16, 128), BF16),
            vmem((NZ, 16, 128), BF16),
            vmem((4, GROUP, D), BF16),
            vmem((4, GROUP, D), BF16),
            dma((5,)), dma((NZ,)), dma((NZ,)), dma((NX, 2)), dma((NX, 2)), dma((4,)), dma((4,)),
            dma((4,)), dma((4,)), dma((4, 2)), dma((NX, 2)), dma((NZ,)), dma((NZ,)), dma((4,)), dma((4,)),
        ],
        compiler_params=pltpu.CompilerParams(
            collective_id=1, has_side_effects=True, vmem_limit_bytes=48 * 1024 * 1024
        ),
        name="pooling_grads",
    )(texts, frames, frame_mask, cotangent.T)


def solution(mesh):
    return jax.shard_map(
        per_device,
        mesh=mesh,
        in_specs=(P(("blk", "rep"), None), P("blk", None, None), P("blk", None), P(None, "blk")),
        out_specs=(P(("blk", "rep"), None), P(("blk", "rep"), None, None)),
        check_vma=False,
    )
```

time: 1160 us -> 58.1 us (0.05)
  blocking collectives: 1030 us -> 0 us
  matrix products: 78.6 us -> 0 us
  Pallas kernels: 0 us -> 52.5 us
  other arithmetic: 22.5 us -> 0 us
  between operations: 14.7 us -> 0.65 us
    unnamed x1 -> x0, blocking collectives: 794 us -> none
    all_gather x1 -> x0, blocking collectives: 233 us -> none  [per_device(): gathered = lax.all_gather(texts, 'blk', axis=0, tiled=True)]
    dot_general x48 -> x0, matrix products: 78.6 us -> none  [the longest x8 31.3 us: pair_block(): jnp.einsum('tcf,tcd->cfd', probs_low, pooled_low, preferred_element_type=...]
    pallas_call x0 -> x1, Pallas kernels: none -> 52.5 us  [per_device(): pl.pallas_call(kernel, out_shape=(jax.ShapeDtypeStruct((ROWS, D), BF16),...]
  transfers between devices with their start and end apart: 1 -> 0, of which waited for: 0 -> 0; matrix products, arithmetic and copies ran while one was open for 0% -> 0% of each run, Pallas kernels for 0% -> 0%
where the time goes in v1:
time: 58.1 us; the launch traced here: 57.8 us
  Pallas kernels  52.5 us (90%)
  local copies, waits for them, and re-layouts  4.68 us (8%)
  between operations  0.65 us (1%)
    pallas_call x1, Pallas kernels, per_device(): pl.pallas_call(kernel, out_shape=(jax.ShapeDtypeStruct((ROWS, D), BF16),...  52.5 us
    unnamed x10, local copies, waits for them, and re-layouts  4.68 us

profile of v1, /device:TPU:1, one launch (start us, length us, event | category | flops | bytes accessed | tf_op | source)
XLA Modules:
  0.0 57.8 jit_solution(2261171934721469896)
XLA Ops:
  0.6 0.0 copy-start
  0.6 1.1 %copy-done = bf16[16,48,512]{2,1,0:T(8,128)(2,1)S(1)} copy-done((bf16[16,48,512]{2,1,0:T(8,128)(2,1)S(1)}, bf16[16,48,512]{2,1,0:T(8,128)(2,1)}, u32[]{:S(2)}) %copy-start) | copy-done | bytes 786456
  1.8 0.0 copy-start.1
  1.8 0.9 %copy-done.1 = f32[2048,16]{0,1:T(8,128)S(1)} copy-done((f32[2048,16]{0,1:T(8,128)S(1)}, f32[2048,16]{0,1:T(8,128)}, u32[]{:S(2)}) %copy-start.1) | copy-done | bytes 131096
  2.7 0.0 copy-start.2
  2.7 0.7 %copy-done.2 = s32[16,48]{1,0:T(8,128)S(1)} copy-done((s32[16,48]{1,0:T(8,128)S(1)}, s32[16,48]{1,0:T(8,128)}, u32[]{:S(2)}) %copy-start.2) | copy-done | bytes 3096
  3.4 0.0 copy-start.3
  3.4 0.7 %copy-done.3 = bf16[4,512]{1,0:T(4,128)(2,1)S(1)} copy-done((bf16[4,512]{1,0:T(4,128)(2,1)S(1)}, bf16[4,512]{1,0:T(4,128)(2,1)}, u32[]{:S(2)}) %copy-start.3) | copy-done | bytes 4120
  4.1 52.5 %pooling_grads.1 = (bf16[4,512]{1,0:T(4,128)(2,1)S(1)}, bf16[4,48,512]{2,1,0:T(8,128)(2,1)S(1)}) custom-call(bf16[4,512]{1,0:T(4,128)(2,1)S(1)} %copy-done.3, bf16[16,48,512]{2,1,0:T(8,128)(2,1)S(1)} %copy-done, s32[16,48]{1,0:T(8,128)S(1)} %copy-done.2, f32[16,2048]{1,0:T(8,128)S(1)} %bitcast.1), custom_call_target="tpu_custom_call" | custom-call | tf_op jit(solution)/shard_map/pooling_grads/pallas_call | solution.py:357
  56.5 0.6 %copy.8 = bf16[4,512]{1,0:T(4,128)(2,1)} copy(bf16[4,512]{1,0:T(4,128)(2,1)S(1)} %get-tuple-element.4) | data formatting | bytes 8192
  57.1 0.7 %copy.9 = bf16[4,48,512]{2,1,0:T(8,128)(2,1)} copy(bf16[4,48,512]{2,1,0:T(8,128)(2,1)S(1)} %get-tuple-element.5) | data formatting | bytes 393216
Async XLA Ops:
  0.6 1.1 %copy-start = (bf16[16,48,512]{2,1,0:T(8,128)(2,1)S(1)}, bf16[16,48,512]{2,1,0:T(8,128)(2,1)}, u32[]{:S(2)}) copy-start(bf16[16,48,512]{2,1,0:T(8,128)(2,1)} %frames_ref.1) | copy-start | bytes 2359300
  1.8 0.9 %copy-start.1 = (f32[2048,16]{0,1:T(8,128)S(1)}, f32[2048,16]{0,1:T(8,128)}, u32[]{:S(2)}) copy-start(f32[2048,16]{0,1:T(8,128)} %param.7) | copy-start | bytes 393220
  2.7 0.7 %copy-start.2 = (s32[16,48]{1,0:T(8,128)S(1)}, s32[16,48]{1,0:T(8,128)}, u32[]{:S(2)}) copy-start(s32[16,48]{1,0:T(8,128)} %mask_ref.1) | copy-start | bytes 9220
  3.4 0.7 %copy-start.3 = (bf16[4,512]{1,0:T(4,128)(2,1)S(1)}, bf16[4,512]{1,0:T(4,128)(2,1)}, u32[]{:S(2)}) copy-start(bf16[4,512]{1,0:T(4,128)(2,1)} %texts_ref.1) | copy-start | bytes 12292

commit v2 on v1

v2 whole, which is shorter than its diff:
```python
import math

import jax
import jax.numpy as jnp
from jax import lax
from jax.experimental import pallas as pl
from jax.experimental.pallas import tpu as pltpu
from jax.sharding import PartitionSpec as P

MESH = pl.DeviceIdType.MESH
EPSILON = 1e-05
NX, NZ, NY = 4, 8, 8
D, FR, C_DEV, ROWS = 512, 48, 16, 4
CHUNK = 128
GROUP = 192
VMEM_LIMIT = 48 * 1024 * 1024
FACTOR = 1.0 / math.sqrt(D)
F32, BF16 = jnp.float32, jnp.bfloat16


def dot(a, b, ca, cb):
    return lax.dot_general(a, b, (((ca,), (cb,)), ((), ())), preferred_element_type=F32)


def swap(v):
    return pltpu.roll(v, 4, axis=1)


def tiles_to_rows(tiles):
    n = tiles.shape[0]
    pairs = tiles.reshape(n // 2, 2, 16, 128)
    low = lax.broadcasted_iota(jnp.int32, (n // 2, 8, 128), 1) < 4
    out = []
    for half in range(2):
        a = pairs[:, 0, 8 * half : 8 * half + 8]
        b = pairs[:, 1, 8 * half : 8 * half + 8]
        out.append(jnp.where(low, a, swap(b)).reshape(4 * n, 128))
        out.append(jnp.where(low, swap(a), b).reshape(4 * n, 128))
    return out


def rows_to_tiles(rows):
    n = rows.shape[0] // 4
    low = lax.broadcasted_iota(jnp.int32, (n // 2, 8, 128), 1) < 4
    blocks = [rows[:, 128 * k : 128 * k + 128].reshape(n // 2, 8, 128) for k in range(4)]
    first, second = [], []
    for half in range(2):
        a, b = blocks[2 * half], blocks[2 * half + 1]
        first.append(jnp.where(low, a, swap(b)))
        second.append(jnp.where(low, swap(a), b))
    first = jnp.concatenate(first, axis=1)
    second = jnp.concatenate(second, axis=1)
    return jnp.stack([first, second], axis=1).reshape(n, 16, 128)


def kernel(
    texts_ref, frames_ref, mask_ref, cot_ref, text_out, frame_out,
    frames, cot, tile, texts_in, texts, cot_sel, counts, gram_hi, gram_lo,
    probs_low, weights, scaled, text_tiles, core_send, core_recv, home_send, home_recv,
    frame_send, frame_recv,
    load_sem, ag_xy_send, ag_xy_recv, ag_z_send, ag_z_recv, ag_c_send, ag_c_recv,
    rs_c_send, rs_c_recv, rs_send, rs_recv, fr_send, fr_recv,
):
    blk, rep = lax.axis_index("blk"), lax.axis_index("rep")
    core = blk % 2
    y = (blk // 2) % 2 * 4 + rep
    z = blk // 4 % NZ
    x = blk // 32
    odd, half = y % 2, y // 2
    parity = half % 2
    handlers = ((2 * half + 1 - parity) % NY, (2 * half + NY - 1 + 3 * parity) % NY)
    pair = (half + parity + odd + 3) % 4
    slot = (half + 1 - odd) % 2
    own = slot == 0

    def device(xx, zz, yy, cc):
        return (((xx * NZ + zz) * 2 + yy // 4) * 2 + cc, yy % 4)

    sibling = device(x, z, y, 1 - core)

    def send(src, dst, send_sem, recv_sem, to):
        return pltpu.make_async_remote_copy(
            src_ref=src, dst_ref=dst, send_sem=send_sem, recv_sem=recv_sem, device_id=to, device_id_type=MESH
        )

    started = []

    def start(copy, when=None):
        started.append((copy, when))
        if when is None:
            copy.start()
        else:
            pl.when(when)(copy.start)

    def drain():
        for copy, when in started:
            if when is None:
                copy.wait_send()
            else:
                pl.when(when)(copy.wait_send)

    def arrived(ref, sem):
        pltpu.make_async_copy(ref, ref, sem).wait()

    loads = [pltpu.make_async_copy(cot_ref, cot, load_sem.at[4])]
    for g in range(4):
        loads.append(pltpu.make_async_copy(frames_ref.at[pl.ds(4 * g, 4)], frames.at[pl.ds(4 * g, 4)], load_sem.at[g]))
    for load in loads:
        load.start()

    barrier = pltpu.get_barrier_semaphore()

    def greet(to):
        pl.semaphore_signal(barrier, inc=1, device_id=to, device_id_type=MESH)

    greet(sibling)
    for dz in (4, 3, 5, 2, 6, 1, 7):
        greet(device(x, (z + dz) % NZ, y, core))
    for dx in (2, 1, 3, 0):
        xx = (x + dx) % NX
        for h in range(2):
            if dx == 0 and h == 0:

                @pl.when(jnp.logical_not(own))
                def _():
                    greet(device(x, z, handlers[0], core))
                    greet(device(x, z, 2 * pair + odd, core))

                greet(device(x, z, 2 * pair + 1 - odd, core))
            else:
                greet(device(xx, z, handlers[h], core))
                if dx > 0:
                    greet(device(xx, z, 2 * pair + h, core))
    for k in range(1, 4):
        greet((blk, (rep + k) % 4))

    rows = texts_ref[...].astype(F32)
    tile[...] = jnp.concatenate([rows[:, 128 * k : 128 * k + 128] for k in range(4)], axis=0).astype(BF16)

    @pl.when(own)
    def _():
        pl.semaphore_wait(barrier, 1 + 7 + 3 + 16 - 2)

    @pl.when(jnp.logical_not(own))
    def _():
        pl.semaphore_wait(barrier, 1 + 7 + 3 + 16)

    mine = texts_in.at[z, core, 2 * x + odd]

    @pl.when(own)
    def _():
        pltpu.make_async_copy(tile, mine, ag_xy_recv).start()

    for dx in (2, 1, 3, 0):
        for h in range(2):
            to = device((x + dx) % NX, z, handlers[h], core)
            copy = send(tile, mine, ag_xy_send.at[dx, h], ag_xy_recv, to)
            start(copy, jnp.logical_not(own) if dx == 0 and h == 0 else None)

    loads[0].wait()
    picked = lax.broadcasted_iota(jnp.int32, (512, CHUNK), 0)
    lane = lax.broadcasted_iota(jnp.int32, (512, CHUNK), 1)
    wanted = (
        lane // 8 % 4 * 128 + lane // 64 * 64 + pair // 2 * 32 + lane // 32 % 2 * 16 + pair % 2 * 8 + lane % 8
    )
    choose = jnp.where(picked == wanted, 1.0, 0.0).astype(BF16)
    for k in range(4):
        wide = jnp.concatenate([cot[:, 512 * i + 128 * k : 512 * i + 128 * k + 128] for i in range(NX)], axis=1)
        high = wide.astype(BF16)
        low = (wide - high.astype(F32)).astype(BF16)
        cot_sel[k] = dot(high, choose, 1, 0) + dot(low, choose, 1, 0)
    totals = jnp.sum(mask_ref[...].astype(F32), axis=1, keepdims=True)
    counts[...] = jnp.broadcast_to(totals, (C_DEV, CHUNK))

    plane = texts_in.at[z, core]
    arrived(plane, ag_xy_recv)
    for dz in (4, 3, 5, 2, 6, 1, 7):
        start(send(plane, plane, ag_z_send.at[dz], ag_z_recv.at[z], device(x, (z + dz) % NZ, y, core)))

    same = (
        lax.broadcasted_iota(jnp.int32, (GROUP, GROUP), 0) // FR
        == lax.broadcasted_iota(jnp.int32, (GROUP, GROUP), 1) // FR
    )

    def group_frames(g):
        return frames[4 * g : 4 * g + 4].reshape(GROUP, D)

    for g in range(4):
        loads[1 + g].wait()
        block = group_frames(g)
        gram = jnp.where(same, dot(block, block, 1, 1), 0.0)
        high = gram.astype(BF16)
        gram_hi[g] = high
        gram_lo[g] = (gram - high.astype(F32)).astype(BF16)

    def share(k):
        for zz in (2 * k, 2 * k + 1):

            @pl.when(z != zz)
            def _():
                arrived(texts_in.at[zz, core], ag_z_recv.at[zz])

        both = texts_in.at[pl.ds(2 * k, 2), core]
        start(send(both, both, ag_c_send.at[k], ag_c_recv.at[k], sibling))

    def work(k):
        arrived(texts_in.at[pl.ds(2 * k, 2), 1 - core], ag_c_recv.at[k])
        columns = slice(CHUNK * k, CHUNK * k + CHUNK)
        tiles = texts_in[2 * k : 2 * k + 2].reshape(32, 16, 128).astype(F32)
        for i, block in enumerate(tiles_to_rows(tiles)):
            texts[columns, 128 * i : 128 * i + 128] = block.astype(BF16)
        chunk = texts[columns, :]
        cot_rows = cot_sel[k]
        frame_index = lax.broadcasted_iota(jnp.int32, (FR, CHUNK), 0).astype(F32)
        for g in range(4):
            scores = dot(group_frames(g), chunk, 1, 1)
            kept = []
            for q in range(4):
                raw = scores[FR * q : FR * q + FR]
                live = frame_index < counts[4 * g + q : 4 * g + q + 1, :]
                masked = jnp.where(live, raw * FACTOR, -1e30)
                top = jnp.max(masked, axis=0, keepdims=True)
                grown = jnp.exp(masked - top)
                probs = grown * (1.0 / jnp.sum(grown, axis=0, keepdims=True))
                low = probs.astype(BF16)
                kept.append((raw, probs, low))
            group_low = jnp.concatenate([low for _, _, low in kept], axis=0)
            rows = slice(GROUP * g, GROUP * g + GROUP)
            probs_low[rows, columns] = group_low
            against = dot(gram_hi[g], group_low, 1, 0) + dot(gram_lo[g], group_low, 1, 0)
            for q in range(4):
                raw, probs, low = kept[q]
                low = low.astype(F32)
                with_pooled = against[FR * q : FR * q + FR]
                square = jnp.maximum(jnp.sum(low * with_pooled, axis=0, keepdims=True), 0.0)
                inner = jnp.sum(low * raw, axis=0, keepdims=True)
                inverse = lax.rsqrt(square * (1.0 / D) + EPSILON)
                up = inverse * cot_rows[4 * g + q : 4 * g + q + 1, :] * FACTOR
                back = up * inverse * inverse * inner * (1.0 / D)
                prob_grad = up * raw - back * with_pooled
                centred = jnp.sum(probs * prob_grad, axis=0, keepdims=True)
                score_grad = probs * (prob_grad - centred)
                at = slice(GROUP * g + FR * q, GROUP * g + FR * q + FR)
                weights[at, columns] = (up * low + FACTOR * score_grad).astype(BF16)
                scaled[at, columns] = (back * low).astype(BF16)
        part = dot(weights[:, columns], frames[...].reshape(C_DEV * FR, D), 0, 0)
        text_tiles[k] = rows_to_tiles(part).reshape(2, 2, 8, 16, 128)
        core_send[k] = text_tiles[k, :, 1 - core].astype(BF16)
        start(send(core_send.at[k], core_recv.at[k], rs_c_send.at[k], rs_c_recv.at[k], sibling))

    def combine(k):
        arrived(core_recv.at[k], rs_c_recv.at[k])
        home_send[k] = (text_tiles[k, :, core] + core_recv[k].astype(F32)).astype(BF16)
        landing = home_recv.at[(x * NZ + z) * 2 + slot]
        for dx in (2, 1, 3, 0):
            xx = (x + dx) % NX
            for rr in range(2):
                for zz in range(2):
                    block = home_send.at[k, zz, 2 * xx + rr]
                    to = device(xx, 2 * k + zz, 2 * pair + rr, core)
                    copy = send(block, landing, rs_send.at[k, dx, rr, zz], rs_recv, to)
                    if dx == 0:
                        stays = jnp.logical_and(jnp.logical_and(own, odd == rr), z == 2 * k + zz)

                        @pl.when(stays)
                        def _():
                            pltpu.make_async_copy(block, landing, rs_recv).start()

                        start(copy, jnp.logical_not(stays))
                    else:
                        start(copy)

    share(0)
    share(1)
    work(0)
    share(2)
    work(1)
    combine(0)
    share(3)
    work(2)
    combine(1)
    work(3)
    combine(2)

    for g in range(4):
        rows = slice(GROUP * g, GROUP * g + GROUP)
        mixed = jnp.where(same, dot(scaled[rows, :], probs_low[rows, :], 1, 1), 0.0)
        grad = dot(weights[rows, :], texts[...], 1, 0) - dot(mixed.astype(BF16), group_frames(g), 1, 0)
        frame_send[g] = grad.astype(BF16)
        start(send(frame_send.at[g], frame_recv.at[rep], fr_send.at[g], fr_recv.at[rep], (blk, g)), rep != g)
        if g == 0:
            combine(3)

    total = frame_send[rep].astype(F32)
    for k in range(1, 4):
        source = (rep + k) % 4
        arrived(frame_recv.at[source], fr_recv.at[source])
        total = total + frame_recv[source].astype(F32)
    frame_out[...] = total.astype(BF16).reshape(4, FR, D)

    arrived(home_recv, rs_recv)
    summed = jnp.sum(home_recv[...].astype(F32), axis=0)
    text_out[...] = jnp.concatenate([summed[4 * k : 4 * k + 4] for k in range(4)], axis=1).astype(BF16)
    drain()


def per_device(texts, frames, frame_mask, cotangent):
    vmem, dma = pltpu.VMEM, pltpu.SemaphoreType.DMA
    whole = pl.BlockSpec(memory_space=pltpu.VMEM)
    remote = pl.BlockSpec(memory_space=pl.ANY)
    clip_rows = C_DEV * FR
    return pl.pallas_call(
        kernel,
        out_shape=(
            jax.ShapeDtypeStruct((ROWS, D), BF16),
            jax.ShapeDtypeStruct((4, FR, D), BF16),
        ),
        in_specs=[whole, remote, whole, remote],
        out_specs=(whole, whole),
        scratch_shapes=[
            vmem((C_DEV, FR, D), BF16),
            vmem((C_DEV, 2048), F32),
            vmem((16, 128), BF16),
            vmem((NZ, 2, 8, 16, 128), BF16),
            vmem((4 * CHUNK, D), BF16),
            vmem((4, C_DEV, CHUNK), F32),
            vmem((C_DEV, CHUNK), F32),
            vmem((4, GROUP, GROUP), BF16),
            vmem((4, GROUP, GROUP), BF16),
            vmem((clip_rows, 4 * CHUNK), BF16),
            vmem((clip_rows, 4 * CHUNK), BF16),
            vmem((clip_rows, 4 * CHUNK), BF16),
            vmem((4, 2, 2, 8, 16, 128), F32),
            vmem((4, 2, 8, 16, 128), BF16),
            vmem((4, 2, 8, 16, 128), BF16),
            vmem((4, 2, 8, 16, 128), BF16),
            vmem((64, 16, 128), BF16),
            vmem((4, GROUP, D), BF16),
            vmem((4, GROUP, D), BF16),
            dma((5,)), dma((NX, 2)), dma, dma((NZ,)), dma((NZ,)), dma((4,)), dma((4,)),
            dma((4,)), dma((4,)), dma((4, NX, 2, 2)), dma, dma((4,)), dma((4,)),
        ],
        compiler_params=pltpu.CompilerParams(
            collective_id=1, has_side_effects=True, vmem_limit_bytes=VMEM_LIMIT
        ),
        name="pooling_grads",
    )(*[pltpu.with_memory_space_constraint(v, pltpu.HBM) for v in (texts, frames, frame_mask, cotangent.T)])


def solution(mesh):
    return jax.shard_map(
        per_device,
        mesh=mesh,
        in_specs=(P(("blk", "rep"), None), P("blk", None, None), P("blk", None), P(None, "blk")),
        out_specs=(P(("blk", "rep"), None), P(("blk", "rep"), None, None)),
        check_vma=False,
    )
```

time: 58.1 us -> 53.8 us (0.926)
  the two profiles are of different devices: /device:TPU:1 before, /device:TPU:56 now
where the time goes in v2:
time: 53.8 us; the launch traced here: 53.6 us
  Pallas kernels  51.7 us (96%)
  local copies, waits for them, and re-layouts  1.27 us (2%)
  between operations  0.64 us (1%)
    pallas_call x1, Pallas kernels, per_device(): pl.pallas_call(kernel, out_shape=(jax.ShapeDtypeStruct((ROWS, D), BF16),...  51.7 us
    unnamed x2, local copies, waits for them, and re-layouts  1.27 us

profile of v2, /device:TPU:56, one launch (start us, length us, event | category | flops | bytes accessed | tf_op | source)
XLA Modules:
  0.0 53.6 jit_solution(13517283856068475815)
XLA Ops:
  0.6 51.7 %pooling_grads.1 = (bf16[4,512]{1,0:T(4,128)(2,1)S(1)}, bf16[4,48,512]{2,1,0:T(8,128)(2,1)S(1)}) custom-call(bf16[4,512]{1,0:T(4,128)(2,1)} %texts_ref.1, bf16[16,48,512]{2,1,0:T(8,128)(2,1)} %frames_ref.1, s32[16,48]{1,0:T(8,128)} %mask_ref.1, f32[16,2048]{1,0:T(8,128)} %bitcast.1), custom_call_target="tpu_custom_call" | custom-call | tf_op jit(solution)/shard_map/pooling_grads/pallas_call | solution.py:312
  52.3 0.6 %copy.8 = bf16[4,512]{1,0:T(4,128)(2,1)} copy(bf16[4,512]{1,0:T(4,128)(2,1)S(1)} %get-tuple-element.4) | data formatting | bytes 8192
  52.9 0.7 %copy.9 = bf16[4,48,512]{2,1,0:T(8,128)(2,1)} copy(bf16[4,48,512]{2,1,0:T(8,128)(2,1)S(1)} %get-tuple-element.5) | data formatting | bytes 393216

commit v3 on v2

v3 whole, which is shorter than its diff:
```python
import math

import jax
import jax.numpy as jnp
from jax import lax
from jax.experimental import pallas as pl
from jax.experimental.pallas import tpu as pltpu
from jax.sharding import PartitionSpec as P

MESH = pl.DeviceIdType.MESH
EPSILON = 1e-05
FAR_Z = (4, 3, 5, 2, 6, 1, 7, 0)
FAR_X = (2, 1, 3)
NX, NZ, NY = 4, 8, 8
D, FR, C_DEV, ROWS = 512, 48, 16, 4
CHUNK = 256
GROUP = 192
VMEM_LIMIT = 48 * 1024 * 1024
FACTOR = 1.0 / math.sqrt(D)
F32, BF16 = jnp.float32, jnp.bfloat16


def dot(a, b, ca, cb):
    return lax.dot_general(a, b, (((ca,), (cb,)), ((), ())), preferred_element_type=F32)


def swap(v):
    return pltpu.roll(v, 4, axis=1)


def tiles_to_rows(tiles):
    n = tiles.shape[0]
    pairs = tiles.reshape(n // 2, 2, 16, 128)
    low = lax.broadcasted_iota(jnp.int32, (n // 2, 8, 128), 1) < 4
    out = []
    for half in range(2):
        a = pairs[:, 0, 8 * half : 8 * half + 8]
        b = pairs[:, 1, 8 * half : 8 * half + 8]
        out.append(jnp.where(low, a, swap(b)).reshape(4 * n, 128))
        out.append(jnp.where(low, swap(a), b).reshape(4 * n, 128))
    return out


def rows_to_tiles(rows):
    n = rows.shape[0] // 4
    low = lax.broadcasted_iota(jnp.int32, (n // 2, 8, 128), 1) < 4
    blocks = [rows[:, 128 * k : 128 * k + 128].reshape(n // 2, 8, 128) for k in range(4)]
    first, second = [], []
    for half in range(2):
        a, b = blocks[2 * half], blocks[2 * half + 1]
        first.append(jnp.where(low, a, swap(b)))
        second.append(jnp.where(low, swap(a), b))
    first = jnp.concatenate(first, axis=1)
    second = jnp.concatenate(second, axis=1)
    return jnp.stack([first, second], axis=1).reshape(n, 16, 128)


def kernel(
    texts_ref, frames_ref, mask_ref, cot_ref, text_out, frame_out,
    frames, cot, tile, texts_in, texts, cot_sel, counts, gram_hi, gram_lo,
    probs_low, weights, scaled, text_tiles, core_send, core_recv, x_send, x_recv, home_send, home_recv,
    frame_send, frame_recv,
    load_sem, ag_send, ag_recv, ag_x_send, ag_x_recv, ag_c_send, ag_c_recv,
    rs_c_send, rs_c_recv, rs_x_send, rs_x_recv, rs_send, rs_recv, fr_send, fr_recv,
):
    blk, rep = lax.axis_index("blk"), lax.axis_index("rep")
    core = blk % 2
    high = blk // 2 % 2
    y = high * 4 + rep
    z = blk // 4 % NZ
    x = blk // 32
    inner = (rep + 1) // 2 % 2
    side = (high + 1 + inner) % 2
    clips = rep // 2 * 8
    place = rep % 2
    handlers = (4 * high + 1, 4 * high + 2, 4 - 4 * high, 7 - 4 * high)
    peers = tuple(4 * side + k for k in range(4)) + (4 - 4 * side + 1 - inner, 4 - 4 * side + 2 + inner)

    def device(xx, zz, yy, cc):
        return (((xx * NZ + zz) * 2 + yy // 4) * 2 + cc, yy % 4)

    sibling = device(x, z, y, 1 - core)
    partner = (blk, rep + 1 - 2 * place)

    def send(src, dst, send_sem, recv_sem, to):
        return pltpu.make_async_remote_copy(
            src_ref=src, dst_ref=dst, send_sem=send_sem, recv_sem=recv_sem, device_id=to, device_id_type=MESH
        )

    started = []

    def start(copy, when=None):
        started.append((copy, when))
        if when is None:
            copy.start()
        else:
            pl.when(when)(copy.start)

    def drain():
        for copy, when in started:
            if when is None:
                copy.wait_send()
            else:
                pl.when(when)(copy.wait_send)

    def arrived(ref, sem):
        pltpu.make_async_copy(ref, ref, sem).wait()

    loads = [pltpu.make_async_copy(cot_ref.at[pl.ds(clips, 8)], cot, load_sem.at[2])]
    for g in range(2):
        loads.append(
            pltpu.make_async_copy(
                frames_ref.at[pl.ds(clips + 4 * g, 4)], frames.at[pl.ds(4 * g, 4)], load_sem.at[g]
            )
        )
    for load in loads:
        load.start()

    barrier = pltpu.get_barrier_semaphore()

    def greet(to):
        pl.semaphore_signal(barrier, inc=1, device_id=to, device_id_type=MESH)

    for dz in FAR_Z:
        for k, yy in enumerate(peers):
            to = device(x, (z + dz) % NZ, yy, core)
            if dz == 0 and k < 4:
                pl.when(yy != y)(lambda to=to: greet(to))
            else:
                greet(to)
    for dx in FAR_X:
        greet(device((x + dx) % NX, z, y, core))
    greet(sibling)

    rows = texts_ref[...].astype(F32)
    tile[...] = jnp.concatenate([rows[:, 128 * k : 128 * k + 128] for k in range(4)], axis=0).astype(BF16)

    @pl.when(inner == 1)
    def _():
        pl.semaphore_wait(barrier, 8 * 6 + 3 + 1 - 1)

    @pl.when(inner == 0)
    def _():
        pl.semaphore_wait(barrier, 8 * 6 + 3 + 1)

    mine = texts_in.at[z, core, x, rep]
    for dz in FAR_Z:
        for k, yy in enumerate(handlers):
            copy = send(tile, mine, ag_send.at[dz, k], ag_recv.at[z], device(x, (z + dz) % NZ, yy, core))
            start(copy, yy != y if dz == 0 and k < 2 else None)

    @pl.when(inner == 1)
    def _():
        pltpu.make_async_copy(tile, mine, ag_recv.at[z]).start()

    loads[0].wait()
    picked = lax.broadcasted_iota(jnp.int32, (512, CHUNK), 0)
    lane = lax.broadcasted_iota(jnp.int32, (512, CHUNK), 1)
    wanted = lane // 16 % 4 * 128 + lane // 128 * 64 + side * 32 + lane // 64 % 2 * 16 + lane % 16
    choose = jnp.where(picked == wanted, 1.0, 0.0).astype(BF16)
    for k in range(4):
        wide = jnp.concatenate([cot[:, 512 * i + 128 * k : 512 * i + 128 * k + 128] for i in range(NX)], axis=1)
        upper = wide.astype(BF16)
        lower = (wide - upper.astype(F32)).astype(BF16)
        both = dot(jnp.concatenate([upper, lower], axis=0), choose, 1, 0)
        cot_sel[k] = both[:8] + both[8:]
    totals = jnp.sum(mask_ref[pl.ds(clips, 8), :].astype(F32), axis=1, keepdims=True)
    counts[...] = jnp.broadcast_to(totals, (8, CHUNK))
    same = (
        lax.broadcasted_iota(jnp.int32, (GROUP, GROUP), 0) // FR
        == lax.broadcasted_iota(jnp.int32, (GROUP, GROUP), 1) // FR
    )

    def group_frames(g):
        return frames[pl.ds(4 * g, 4)].reshape(GROUP, D)

    for g in range(2):
        loads[1 + g].wait()
        block = group_frames(g)
        gram = jnp.where(same, dot(block, block, 1, 1), 0.0)
        upper = gram.astype(BF16)
        gram_hi[g] = upper
        gram_lo[g] = (gram - upper.astype(F32)).astype(BF16)

    def spread(k):
        for zz in (2 * k, 2 * k + 1):
            arrived(texts_in.at[zz, core, x], ag_recv.at[zz])
        line = texts_in.at[pl.ds(2 * k, 2), core, x]
        for dx in FAR_X:
            start(send(line, line, ag_x_send.at[k, dx], ag_x_recv.at[k, x], device((x + dx) % NX, z, y, core)))

    def share(k):
        for dx in FAR_X:
            xx = (x + dx) % NX
            arrived(texts_in.at[pl.ds(2 * k, 2), core, xx], ag_x_recv.at[k, xx])
        both = texts_in.at[pl.ds(2 * k, 2), core]
        start(send(both, both, ag_c_send.at[k], ag_c_recv.at[k], sibling))

    def work(k):
        arrived(texts_in.at[pl.ds(2 * k, 2), 1 - core], ag_c_recv.at[k])
        columns = slice(CHUNK * k, CHUNK * k + CHUNK)
        tiles = texts_in[2 * k : 2 * k + 2].reshape(64, 16, 128).astype(F32)
        for i, block in enumerate(tiles_to_rows(tiles)):
            texts[columns, 128 * i : 128 * i + 128] = block.astype(BF16)
        chunk = texts[columns, :]
        cot_rows = cot_sel[k]
        frame_index = lax.broadcasted_iota(jnp.int32, (FR, CHUNK), 0).astype(F32)
        for g in range(2):
            scores = dot(group_frames(g), chunk, 1, 1)
            kept = []
            for q in range(4):
                raw = scores[FR * q : FR * q + FR]
                live = frame_index < counts[4 * g + q : 4 * g + q + 1, :]
                masked = jnp.where(live, raw * FACTOR, -1e30)
                top = jnp.max(masked, axis=0, keepdims=True)
                grown = jnp.exp(masked - top)
                probs = grown * (1.0 / jnp.sum(grown, axis=0, keepdims=True))
                low = probs.astype(BF16)
                kept.append((raw, probs, low))
            group_low = jnp.concatenate([low for _, _, low in kept], axis=0)
            probs_low[g, :, columns] = group_low
            against = dot(gram_hi[g], group_low, 1, 0) + dot(gram_lo[g], group_low, 1, 0)
            for q in range(4):
                raw, probs, low = kept[q]
                low = low.astype(F32)
                with_pooled = against[FR * q : FR * q + FR]
                square = jnp.maximum(jnp.sum(low * with_pooled, axis=0, keepdims=True), 0.0)
                inner_product = jnp.sum(low * raw, axis=0, keepdims=True)
                inverse = lax.rsqrt(square * (1.0 / D) + EPSILON)
                up = inverse * cot_rows[4 * g + q : 4 * g + q + 1, :] * FACTOR
                back = up * inverse * inverse * inner_product * (1.0 / D)
                prob_grad = up * raw - back * with_pooled
                centred = jnp.sum(probs * prob_grad, axis=0, keepdims=True)
                score_grad = probs * (prob_grad - centred)
                at = slice(FR * q, FR * q + FR)
                weights[g, at, columns] = (up * low + FACTOR * score_grad).astype(BF16)
                scaled[g, at, columns] = (back * low).astype(BF16)
        part = dot(weights[:, :, columns].reshape(8 * FR, CHUNK), frames[...].reshape(8 * FR, D), 0, 0)
        text_tiles[k] = rows_to_tiles(part).reshape(2, 2, NX, 4, 16, 128)
        core_send[k] = text_tiles[k, :, 1 - core].astype(BF16)
        start(send(core_send.at[k], core_recv.at[k], rs_c_send.at[k], rs_c_recv.at[k], sibling))

    def combine(k):
        arrived(core_recv.at[k], rs_c_recv.at[k])
        both = (text_tiles[k, :, core] + core_recv[k].astype(F32)).astype(BF16)
        for zz in range(2):
            x_send[k, :, zz] = both[zz]
        for dx in FAR_X:
            xx = (x + dx) % NX
            start(
                send(
                    x_send.at[k, xx], x_recv.at[k, dx - 1], rs_x_send.at[k, dx - 1], rs_x_recv.at[k, dx - 1],
                    device(xx, z, y, core),
                )
            )

    def deliver(k):
        total = x_send[k, x].astype(F32)
        for dx in FAR_X:
            arrived(x_recv.at[k, dx - 1], rs_x_recv.at[k, dx - 1])
            total = total + x_recv[k, dx - 1].astype(F32)
        home_send[k] = total.astype(BF16)
        landing = home_recv.at[z, rep]
        for zz in range(2):
            for m in range(4):
                block = home_send.at[k, zz, m]
                stays = jnp.logical_and(jnp.logical_and(inner == 1, rep == m), z == 2 * k + zz)
                copy = send(block, landing, rs_send.at[k, zz, m], rs_recv, device(x, 2 * k + zz, 4 * side + m, core))
                if m in (1, 2):

                    @pl.when(stays)
                    def _():
                        pltpu.make_async_copy(block, landing, rs_recv).start()

                    start(copy, jnp.logical_not(stays))
                else:
                    start(copy)

    def frame_grad(g):
        mixed = jnp.where(same, dot(scaled[g], probs_low[g], 1, 1), 0.0)
        return dot(weights[g], texts[...], 1, 0) - dot(mixed.astype(BF16), group_frames(g), 1, 0)

    for k in range(4):
        spread(k)
    share(0)
    share(1)
    work(0)
    share(2)
    work(1)
    combine(0)
    share(3)
    work(2)
    combine(1)
    work(3)
    combine(2)
    frame_send[...] = frame_grad(1 - place).astype(BF16)
    deliver(0)
    start(send(frame_send, frame_recv, fr_send, fr_recv, partner))
    combine(3)
    deliver(1)
    total = frame_grad(place)
    deliver(2)
    deliver(3)

    arrived(frame_recv, fr_recv)
    frame_out[...] = (total + frame_recv[...].astype(F32)).astype(BF16).reshape(4, FR, D)

    arrived(home_recv, rs_recv)
    summed = jnp.sum(home_recv[...].reshape(32, 16, 128).astype(F32), axis=0)
    text_out[...] = jnp.concatenate([summed[4 * k : 4 * k + 4] for k in range(4)], axis=1).astype(BF16)
    drain()


def per_device(texts, frames, frame_mask, cotangent):
    vmem, dma = pltpu.VMEM, pltpu.SemaphoreType.DMA
    whole = pl.BlockSpec(memory_space=pltpu.VMEM)
    remote = pl.BlockSpec(memory_space=pl.ANY)
    return pl.pallas_call(
        kernel,
        out_shape=(
            jax.ShapeDtypeStruct((ROWS, D), BF16),
            jax.ShapeDtypeStruct((4, FR, D), BF16),
        ),
        in_specs=[whole, remote, whole, remote],
        out_specs=(whole, whole),
        scratch_shapes=[
            vmem((8, FR, D), BF16),
            vmem((8, 2048), F32),
            vmem((16, 128), BF16),
            vmem((NZ, 2, NX, 4, 16, 128), BF16),
            vmem((4 * CHUNK, D), BF16),
            vmem((4, 8, CHUNK), F32),
            vmem((8, CHUNK), F32),
            vmem((2, GROUP, GROUP), BF16),
            vmem((2, GROUP, GROUP), BF16),
            vmem((2, GROUP, 4 * CHUNK), BF16),
            vmem((2, GROUP, 4 * CHUNK), BF16),
            vmem((2, GROUP, 4 * CHUNK), BF16),
            vmem((4, 2, 2, NX, 4, 16, 128), F32),
            vmem((4, 2, NX, 4, 16, 128), BF16),
            vmem((4, 2, NX, 4, 16, 128), BF16),
            vmem((4, NX, 2, 4, 16, 128), BF16),
            vmem((4, 3, 2, 4, 16, 128), BF16),
            vmem((4, 2, 4, 16, 128), BF16),
            vmem((NZ, 4, 16, 128), BF16),
            vmem((GROUP, D), BF16),
            vmem((GROUP, D), BF16),
            dma((3,)), dma((NZ, 4)), dma((NZ,)), dma((4, NX)), dma((4, NX)), dma((4,)), dma((4,)),
            dma((4,)), dma((4,)), dma((4, 3)), dma((4, 3)), dma((4, 2, 4)), dma, dma, dma,
        ],
        compiler_params=pltpu.CompilerParams(
            collective_id=1, has_side_effects=True, vmem_limit_bytes=VMEM_LIMIT
        ),
        name="pooling_grads",
    )(*[pltpu.with_memory_space_constraint(v, pltpu.HBM) for v in (texts, frames, frame_mask, cotangent.T)])


def solution(mesh):
    return jax.shard_map(
        per_device,
        mesh=mesh,
        in_specs=(P(("blk", "rep"), None), P("blk", None, None), P("blk", None), P(None, "blk")),
        out_specs=(P(("blk", "rep"), None), P(("blk", "rep"), None, None)),
        check_vma=False,
    )
```

time: 53.8 us -> 49.5 us (0.920)
  the two profiles are of different devices: /device:TPU:56 before, /device:TPU:128 now
where the time goes in v3:
time: 49.5 us; the launch traced here: 49.3 us
  Pallas kernels  47.4 us (96%)
  local copies, waits for them, and re-layouts  1.27 us (3%)
  between operations  0.64 us (1%)
    pallas_call x1, Pallas kernels, per_device(): pl.pallas_call(kernel, out_shape=(jax.ShapeDtypeStruct((ROWS, D), BF16),...  47.4 us
    unnamed x2, local copies, waits for them, and re-layouts  1.27 us

profile of v3, /device:TPU:128, one launch (start us, length us, event | category | flops | bytes accessed | tf_op | source)
XLA Modules:
  0.0 49.3 jit_solution(5267271981843718029)
XLA Ops:
  0.6 47.4 %pooling_grads.1 = (bf16[4,512]{1,0:T(4,128)(2,1)S(1)}, bf16[4,48,512]{2,1,0:T(8,128)(2,1)S(1)}) custom-call(bf16[4,512]{1,0:T(4,128)(2,1)} %texts_ref.1, bf16[16,48,512]{2,1,0:T(8,128)(2,1)} %frames_ref.1, s32[16,48]{1,0:T(8,128)} %mask_ref.1, f32[16,2048]{1,0:T(8,128)} %bitcast.1), custom_call_target="tpu_custom_call" | custom-call | tf_op jit(solution)/shard_map/pooling_grads/pallas_call | solution.py:318
  48.1 0.6 %copy.8 = bf16[4,512]{1,0:T(4,128)(2,1)} copy(bf16[4,512]{1,0:T(4,128)(2,1)S(1)} %get-tuple-element.4) | data formatting | bytes 8192
  48.7 0.7 %copy.9 = bf16[4,48,512]{2,1,0:T(8,128)(2,1)} copy(bf16[4,48,512]{2,1,0:T(8,128)(2,1)S(1)} %get-tuple-element.5) | data formatting | bytes 393216

commit v4 on v3

--- a/solution.py
+++ b/solution.py
@@ -13,7 +13,7 @@
 FAR_X = (2, 1, 3)
 NX, NZ, NY = 4, 8, 8
 D, FR, C_DEV, ROWS = 512, 48, 16, 4
-CHUNK = 256
+CHUNK = 128
 GROUP = 192
 VMEM_LIMIT = 48 * 1024 * 1024
 FACTOR = 1.0 / math.sqrt(D)
@@ -58,10 +58,10 @@
 def kernel(
     texts_ref, frames_ref, mask_ref, cot_ref, text_out, frame_out,
     frames, cot, tile, texts_in, texts, cot_sel, counts, gram_hi, gram_lo,
-    probs_low, weights, scaled, text_tiles, core_send, core_recv, x_send, x_recv, home_send, home_recv,
-    frame_send, frame_recv,
-    load_sem, ag_send, ag_recv, ag_x_send, ag_x_recv, ag_c_send, ag_c_recv,
-    rs_c_send, rs_c_recv, rs_x_send, rs_x_recv, rs_send, rs_recv, fr_send, fr_recv,
+    probs_low, weights, scaled, x_send, x_recv, home_send, home_recv,
+    core_send, core_recv, frame_send, frame_recv,
+    load_sem, swap_send, swap_recv, ag_send, ag_recv, ag_x_send, ag_x_recv,
+    rs_x_send, rs_x_recv, rs_send, rs_recv, fr_c_send, fr_c_recv, fr_send, fr_recv,
 ):
     blk, rep = lax.axis_index("blk"), lax.axis_index("rep")
     core = blk % 2
@@ -106,7 +106,7 @@
     def arrived(ref, sem):
         pltpu.make_async_copy(ref, ref, sem).wait()
 
-    loads = [pltpu.make_async_copy(cot_ref.at[pl.ds(clips, 8)], cot, load_sem.at[2])]
+    loads = [pltpu.make_async_copy(cot_ref.at[pl.ds(clips, 8)], cot.at[pl.ds(0, 8)], load_sem.at[2])]
     for g in range(2):
         loads.append(
             pltpu.make_async_copy(
@@ -132,6 +132,9 @@
         greet(device((x + dx) % NX, z, y, core))
     greet(sibling)
 
+    totals = jnp.sum(mask_ref[pl.ds(clips, 8), :].astype(F32), axis=1, keepdims=True)
+    counts[0] = jnp.broadcast_to(totals, (8, CHUNK))
+
     rows = texts_ref[...].astype(F32)
     tile[...] = jnp.concatenate([rows[:, 128 * k : 128 * k + 128] for k in range(4)], axis=0).astype(BF16)
 
@@ -143,7 +146,7 @@
     def _():
         pl.semaphore_wait(barrier, 8 * 6 + 3 + 1)
 
-    mine = texts_in.at[z, core, x, rep]
+    mine = texts_in.at[z, x, rep]
     for dz in FAR_Z:
         for k, yy in enumerate(handlers):
             copy = send(tile, mine, ag_send.at[dz, k], ag_recv.at[z], device(x, (z + dz) % NZ, yy, core))
@@ -153,19 +156,28 @@
     def _():
         pltpu.make_async_copy(tile, mine, ag_recv.at[z]).start()
 
-    loads[0].wait()
+    for load in loads:
+        load.wait()
+    swaps = (
+        (frames.at[pl.ds(0, 8)], frames.at[pl.ds(8, 8)]),
+        (cot.at[pl.ds(0, 8)], cot.at[pl.ds(8, 8)]),
+        (counts.at[0], counts.at[1]),
+    )
+    for k, (src, dst) in enumerate(swaps):
+        start(send(src, dst, swap_send.at[k], swap_recv.at[k], sibling))
+
     picked = lax.broadcasted_iota(jnp.int32, (512, CHUNK), 0)
     lane = lax.broadcasted_iota(jnp.int32, (512, CHUNK), 1)
-    wanted = lane // 16 % 4 * 128 + lane // 128 * 64 + side * 32 + lane // 64 % 2 * 16 + lane % 16
+    wanted = lane // 16 % 4 * 128 + lane // 64 * 64 + side * 32 + core * 16 + lane % 16
     choose = jnp.where(picked == wanted, 1.0, 0.0).astype(BF16)
+    for k, (src, dst) in enumerate(swaps):
+        arrived(dst, swap_recv.at[k])
     for k in range(4):
         wide = jnp.concatenate([cot[:, 512 * i + 128 * k : 512 * i + 128 * k + 128] for i in range(NX)], axis=1)
         upper = wide.astype(BF16)
         lower = (wide - upper.astype(F32)).astype(BF16)
         both = dot(jnp.concatenate([upper, lower], axis=0), choose, 1, 0)
-        cot_sel[k] = both[:8] + both[8:]
-    totals = jnp.sum(mask_ref[pl.ds(clips, 8), :].astype(F32), axis=1, keepdims=True)
-    counts[...] = jnp.broadcast_to(totals, (8, CHUNK))
+        cot_sel[k] = both[:16] + both[16:]
     same = (
         lax.broadcasted_iota(jnp.int32, (GROUP, GROUP), 0) // FR
         == lax.broadcasted_iota(jnp.int32, (GROUP, GROUP), 1) // FR
@@ -174,8 +186,7 @@
     def group_frames(g):
         return frames[pl.ds(4 * g, 4)].reshape(GROUP, D)
 
-    for g in range(2):
-        loads[1 + g].wait()
+    for g in range(4):
         block = group_frames(g)
         gram = jnp.where(same, dot(block, block, 1, 1), 0.0)
         upper = gram.astype(BF16)
@@ -184,33 +195,28 @@
 
     def spread(k):
         for zz in (2 * k, 2 * k + 1):
-            arrived(texts_in.at[zz, core, x], ag_recv.at[zz])
-        line = texts_in.at[pl.ds(2 * k, 2), core, x]
+            arrived(texts_in.at[zz, x], ag_recv.at[zz])
+        line = texts_in.at[pl.ds(2 * k, 2), x]
         for dx in FAR_X:
             start(send(line, line, ag_x_send.at[k, dx], ag_x_recv.at[k, x], device((x + dx) % NX, z, y, core)))
 
-    def share(k):
+    def work(k):
         for dx in FAR_X:
             xx = (x + dx) % NX
-            arrived(texts_in.at[pl.ds(2 * k, 2), core, xx], ag_x_recv.at[k, xx])
-        both = texts_in.at[pl.ds(2 * k, 2), core]
-        start(send(both, both, ag_c_send.at[k], ag_c_recv.at[k], sibling))
-
-    def work(k):
-        arrived(texts_in.at[pl.ds(2 * k, 2), 1 - core], ag_c_recv.at[k])
+            arrived(texts_in.at[pl.ds(2 * k, 2), xx], ag_x_recv.at[k, xx])
         columns = slice(CHUNK * k, CHUNK * k + CHUNK)
-        tiles = texts_in[2 * k : 2 * k + 2].reshape(64, 16, 128).astype(F32)
+        tiles = texts_in[2 * k : 2 * k + 2].reshape(32, 16, 128).astype(F32)
         for i, block in enumerate(tiles_to_rows(tiles)):
             texts[columns, 128 * i : 128 * i + 128] = block.astype(BF16)
         chunk = texts[columns, :]
-        cot_rows = cot_sel[k]
         frame_index = lax.broadcasted_iota(jnp.int32, (FR, CHUNK), 0).astype(F32)
-        for g in range(2):
+        for g in range(4):
             scores = dot(group_frames(g), chunk, 1, 1)
             kept = []
             for q in range(4):
+                c = 4 * g + q
                 raw = scores[FR * q : FR * q + FR]
-                live = frame_index < counts[4 * g + q : 4 * g + q + 1, :]
+                live = frame_index < counts[c // 8, c % 8 : c % 8 + 1, :]
                 masked = jnp.where(live, raw * FACTOR, -1e30)
                 top = jnp.max(masked, axis=0, keepdims=True)
                 grown = jnp.exp(masked - top)
@@ -221,13 +227,14 @@
             probs_low[g, :, columns] = group_low
             against = dot(gram_hi[g], group_low, 1, 0) + dot(gram_lo[g], group_low, 1, 0)
             for q in range(4):
+                c = 4 * g + q
                 raw, probs, low = kept[q]
                 low = low.astype(F32)
                 with_pooled = against[FR * q : FR * q + FR]
                 square = jnp.maximum(jnp.sum(low * with_pooled, axis=0, keepdims=True), 0.0)
                 inner_product = jnp.sum(low * raw, axis=0, keepdims=True)
                 inverse = lax.rsqrt(square * (1.0 / D) + EPSILON)
-                up = inverse * cot_rows[4 * g + q : 4 * g + q + 1, :] * FACTOR
+                up = inverse * cot_sel[k, c : c + 1, :] * FACTOR
                 back = up * inverse * inverse * inner_product * (1.0 / D)
                 prob_grad = up * raw - back * with_pooled
                 centred = jnp.sum(probs * prob_grad, axis=0, keepdims=True)
@@ -235,16 +242,10 @@
                 at = slice(FR * q, FR * q + FR)
                 weights[g, at, columns] = (up * low + FACTOR * score_grad).astype(BF16)
                 scaled[g, at, columns] = (back * low).astype(BF16)
-        part = dot(weights[:, :, columns].reshape(8 * FR, CHUNK), frames[...].reshape(8 * FR, D), 0, 0)
-        text_tiles[k] = rows_to_tiles(part).reshape(2, 2, NX, 4, 16, 128)
-        core_send[k] = text_tiles[k, :, 1 - core].astype(BF16)
-        start(send(core_send.at[k], core_recv.at[k], rs_c_send.at[k], rs_c_recv.at[k], sibling))
-
-    def combine(k):
-        arrived(core_recv.at[k], rs_c_recv.at[k])
-        both = (text_tiles[k, :, core] + core_recv[k].astype(F32)).astype(BF16)
+        part = dot(weights[:, :, columns].reshape(16 * FR, CHUNK), frames[...].reshape(16 * FR, D), 0, 0)
+        blocks = rows_to_tiles(part).astype(BF16).reshape(2, NX, 4, 16, 128)
         for zz in range(2):
-            x_send[k, :, zz] = both[zz]
+            x_send[k, :, zz] = blocks[zz]
         for dx in FAR_X:
             xx = (x + dx) % NX
             start(
@@ -280,26 +281,29 @@
         mixed = jnp.where(same, dot(scaled[g], probs_low[g], 1, 1), 0.0)
         return dot(weights[g], texts[...], 1, 0) - dot(mixed.astype(BF16), group_frames(g), 1, 0)
 
+    def to_sibling(k, g):
+        core_send[k] = frame_grad(2 + g).astype(BF16)
+        start(send(core_send.at[k], core_recv.at[k], fr_c_send.at[k], fr_c_recv.at[k], sibling))
+
+    def from_sibling(k, g):
+        grad = frame_grad(g)
+        arrived(core_recv.at[k], fr_c_recv.at[k])
+        return grad + core_recv[k].astype(F32)
+
     for k in range(4):
         spread(k)
-    share(0)
-    share(1)
     work(0)
-    share(2)
     work(1)
-    combine(0)
-    share(3)
     work(2)
-    combine(1)
     work(3)
-    combine(2)
-    frame_send[...] = frame_grad(1 - place).astype(BF16)
+    to_sibling(0, 1 - place)
     deliver(0)
+    deliver(1)
+    frame_send[...] = from_sibling(0, 1 - place).astype(BF16)
+    deliver(2)
     start(send(frame_send, frame_recv, fr_send, fr_recv, partner))
-    combine(3)
-    deliver(1)
-    total = frame_grad(place)
-    deliver(2)
+    to_sibling(1, place)
+    total = from_sibling(1, place)
     deliver(3)
 
     arrived(frame_recv, fr_recv)
@@ -324,29 +328,28 @@
         in_specs=[whole, remote, whole, remote],
         out_specs=(whole, whole),
         scratch_shapes=[
-            vmem((8, FR, D), BF16),
-            vmem((8, 2048), F32),
+            vmem((16, FR, D), BF16),
+            vmem((16, 2048), F32),
             vmem((16, 128), BF16),
-            vmem((NZ, 2, NX, 4, 16, 128), BF16),
+            vmem((NZ, NX, 4, 16, 128), BF16),
             vmem((4 * CHUNK, D), BF16),
-            vmem((4, 8, CHUNK), F32),
-            vmem((8, CHUNK), F32),
-            vmem((2, GROUP, GROUP), BF16),
-            vmem((2, GROUP, GROUP), BF16),
-            vmem((2, GROUP, 4 * CHUNK), BF16),
-            vmem((2, GROUP, 4 * CHUNK), BF16),
-            vmem((2, GROUP, 4 * CHUNK), BF16),
-            vmem((4, 2, 2, NX, 4, 16, 128), F32),
-            vmem((4, 2, NX, 4, 16, 128), BF16),
-            vmem((4, 2, NX, 4, 16, 128), BF16),
+            vmem((4, 16, CHUNK), F32),
+            vmem((2, 8, CHUNK), F32),
+            vmem((4, GROUP, GROUP), BF16),
+            vmem((4, GROUP, GROUP), BF16),
+            vmem((4, GROUP, 4 * CHUNK), BF16),
+            vmem((4, GROUP, 4 * CHUNK), BF16),
+            vmem((4, GROUP, 4 * CHUNK), BF16),
             vmem((4, NX, 2, 4, 16, 128), BF16),
             vmem((4, 3, 2, 4, 16, 128), BF16),
             vmem((4, 2, 4, 16, 128), BF16),
             vmem((NZ, 4, 16, 128), BF16),
+            vmem((2, GROUP, D), BF16),
+            vmem((2, GROUP, D), BF16),
             vmem((GROUP, D), BF16),
             vmem((GROUP, D), BF16),
-            dma((3,)), dma((NZ, 4)), dma((NZ,)), dma((4, NX)), dma((4, NX)), dma((4,)), dma((4,)),
-            dma((4,)), dma((4,)), dma((4, 3)), dma((4, 3)), dma((4, 2, 4)), dma, dma, dma,
+            dma((3,)), dma((3,)), dma((3,)), dma((NZ, 4)), dma((NZ,)), dma((4, NX)), dma((4, NX)),
+            dma((4, 3)), dma((4, 3)), dma((4, 2, 4)), dma, dma((2,)), dma((2,)), dma, dma,
         ],
         compiler_params=pltpu.CompilerParams(
             collective_id=1, has_side_effects=True, vmem_limit_bytes=VMEM_LIMIT

time: 49.5 us -> 44.4 us (0.90)
  the two profiles are of different devices: /device:TPU:128 before, /device:TPU:1 now
where the time goes in v4:
time: 44.4 us; the launch traced here: 44.1 us
  Pallas kernels  42.2 us (95%)
  local copies, waits for them, and re-layouts  1.27 us (3%)
  between operations  0.64 us (1%)
    pallas_call x1, Pallas kernels, per_device(): pl.pallas_call(kernel, out_shape=(jax.ShapeDtypeStruct((ROWS, D), BF16),...  42.2 us
    unnamed x2, local copies, waits for them, and re-layouts  1.27 us

profile of v4, /device:TPU:1, one launch (start us, length us, event | category | flops | bytes accessed | tf_op | source)
XLA Modules:
  0.0 44.1 jit_solution(12984402309651802036)
XLA Ops:
  0.6 42.2 %pooling_grads.1 = (bf16[4,512]{1,0:T(4,128)(2,1)S(1)}, bf16[4,48,512]{2,1,0:T(8,128)(2,1)S(1)}) custom-call(bf16[4,512]{1,0:T(4,128)(2,1)} %texts_ref.1, bf16[16,48,512]{2,1,0:T(8,128)(2,1)} %frames_ref.1, s32[16,48]{1,0:T(8,128)} %mask_ref.1, f32[16,2048]{1,0:T(8,128)} %bitcast.1), custom_call_target="tpu_custom_call" | custom-call | tf_op jit(solution)/shard_map/pooling_grads/pallas_call | solution.py:322
  42.9 0.6 %copy.8 = bf16[4,512]{1,0:T(4,128)(2,1)} copy(bf16[4,512]{1,0:T(4,128)(2,1)S(1)} %get-tuple-element.4) | data formatting | bytes 8192
  43.5 0.7 %copy.9 = bf16[4,48,512]{2,1,0:T(8,128)(2,1)} copy(bf16[4,48,512]{2,1,0:T(8,128)(2,1)S(1)} %get-tuple-element.5) | data formatting | bytes 393216

commit v5 on v4

--- a/solution.py
+++ b/solution.py
@@ -56,8 +56,8 @@
 
 
 def kernel(
-    texts_ref, frames_ref, mask_ref, cot_ref, text_out, frame_out,
-    frames, cot, tile, texts_in, texts, cot_sel, counts, gram_hi, gram_lo,
+    texts_hbm, frames_ref, mask_hbm, cot_ref, text_out, frame_out,
+    texts_ref, mask_ref, frames, cot, tile, texts_in, texts, cot_sel, counts, gram_hi, gram_lo,
     probs_low, weights, scaled, x_send, x_recv, home_send, home_recv,
     core_send, core_recv, frame_send, frame_recv,
     load_sem, swap_send, swap_recv, ag_send, ag_recv, ag_x_send, ag_x_recv,
@@ -69,12 +69,15 @@
     y = high * 4 + rep
     z = blk // 4 % NZ
     x = blk // 32
-    inner = (rep + 1) // 2 % 2
-    side = (high + 1 + inner) % 2
     clips = rep // 2 * 8
     place = rep % 2
-    handlers = (4 * high + 1, 4 * high + 2, 4 - 4 * high, 7 - 4 * high)
-    peers = tuple(4 * side + k for k in range(4)) + (4 - 4 * side + 1 - inner, 4 - 4 * side + 2 + inner)
+    sign = 1 - 2 * place
+    handlers = (y, (y + NY + 2 * sign) % NY, (y + NY - sign) % NY, (y + NY - 3 * sign) % NY)
+    peers = (y, *((y + NY + k * sign) % NY for k in (-3, -2, 2, -1)))
+    first = (y + 5 * (1 - place)) % NY
+
+    def source(m):
+        return (first + (m + 8 - first) % 4) % NY
 
     def device(xx, zz, yy, cc):
         return (((xx * NZ + zz) * 2 + yy // 4) * 2 + cc, yy % 4)
@@ -113,48 +116,42 @@
                 frames_ref.at[pl.ds(clips + 4 * g, 4)], frames.at[pl.ds(4 * g, 4)], load_sem.at[g]
             )
         )
-    for load in loads:
-        load.start()
-
     barrier = pltpu.get_barrier_semaphore()
 
     def greet(to):
         pl.semaphore_signal(barrier, inc=1, device_id=to, device_id_type=MESH)
 
     for dz in FAR_Z:
-        for k, yy in enumerate(peers):
-            to = device(x, (z + dz) % NZ, yy, core)
-            if dz == 0 and k < 4:
-                pl.when(yy != y)(lambda to=to: greet(to))
-            else:
-                greet(to)
+        for yy in peers[dz == 0 :]:
+            greet(device(x, (z + dz) % NZ, yy, core))
     for dx in FAR_X:
         greet(device((x + dx) % NX, z, y, core))
     greet(sibling)
-
+    greet(partner)
+
+    early = (
+        pltpu.make_async_copy(texts_hbm, texts_ref, load_sem.at[3]),
+        pltpu.make_async_copy(mask_hbm, mask_ref, load_sem.at[4]),
+    )
+    for load in (*early, *loads):
+        load.start()
+    for load in early:
+        load.wait()
     totals = jnp.sum(mask_ref[pl.ds(clips, 8), :].astype(F32), axis=1, keepdims=True)
     counts[0] = jnp.broadcast_to(totals, (8, CHUNK))
 
     rows = texts_ref[...].astype(F32)
     tile[...] = jnp.concatenate([rows[:, 128 * k : 128 * k + 128] for k in range(4)], axis=0).astype(BF16)
 
-    @pl.when(inner == 1)
-    def _():
-        pl.semaphore_wait(barrier, 8 * 6 + 3 + 1 - 1)
-
-    @pl.when(inner == 0)
-    def _():
-        pl.semaphore_wait(barrier, 8 * 6 + 3 + 1)
+    pl.semaphore_wait(barrier, 8 * 5 - 1 + 3 + 1 + 1)
 
     mine = texts_in.at[z, x, rep]
     for dz in FAR_Z:
         for k, yy in enumerate(handlers):
-            copy = send(tile, mine, ag_send.at[dz, k], ag_recv.at[z], device(x, (z + dz) % NZ, yy, core))
-            start(copy, yy != y if dz == 0 and k < 2 else None)
-
-    @pl.when(inner == 1)
-    def _():
-        pltpu.make_async_copy(tile, mine, ag_recv.at[z]).start()
+            if dz > 0 or k > 0:
+                to = device(x, (z + dz) % NZ, yy, core)
+                start(send(tile, mine, ag_send.at[dz, k], ag_recv.at[z], to))
+    pltpu.make_async_copy(tile, mine, ag_recv.at[z]).start()
 
     for load in loads:
         load.wait()
@@ -168,7 +165,8 @@
 
     picked = lax.broadcasted_iota(jnp.int32, (512, CHUNK), 0)
     lane = lax.broadcasted_iota(jnp.int32, (512, CHUNK), 1)
-    wanted = lane // 16 % 4 * 128 + lane // 64 * 64 + side * 32 + core * 16 + lane % 16
+    upper_half = (first + (lane // 4 % 4 + 8 - first) % 4) % NY // 4
+    wanted = lane // 16 % 4 * 128 + lane // 64 * 64 + upper_half * 32 + core * 16 + lane % 16
     choose = jnp.where(picked == wanted, 1.0, 0.0).astype(BF16)
     for k, (src, dst) in enumerate(swaps):
         arrived(dst, swap_recv.at[k])
@@ -265,17 +263,14 @@
         for zz in range(2):
             for m in range(4):
                 block = home_send.at[k, zz, m]
-                stays = jnp.logical_and(jnp.logical_and(inner == 1, rep == m), z == 2 * k + zz)
-                copy = send(block, landing, rs_send.at[k, zz, m], rs_recv, device(x, 2 * k + zz, 4 * side + m, core))
-                if m in (1, 2):
-
-                    @pl.when(stays)
-                    def _():
-                        pltpu.make_async_copy(block, landing, rs_recv).start()
-
-                    start(copy, jnp.logical_not(stays))
-                else:
-                    start(copy)
+                stays = jnp.logical_and(rep == m, z == 2 * k + zz)
+                copy = send(block, landing, rs_send.at[k, zz, m], rs_recv, device(x, 2 * k + zz, source(m), core))
+
+                @pl.when(stays)
+                def _():
+                    pltpu.make_async_copy(block, landing, rs_recv).start()
+
+                start(copy, jnp.logical_not(stays))
 
     def frame_grad(g):
         mixed = jnp.where(same, dot(scaled[g], probs_low[g], 1, 1), 0.0)
@@ -306,13 +301,13 @@
     total = from_sibling(1, place)
     deliver(3)
 
+    drain()
     arrived(frame_recv, fr_recv)
     frame_out[...] = (total + frame_recv[...].astype(F32)).astype(BF16).reshape(4, FR, D)
 
     arrived(home_recv, rs_recv)
     summed = jnp.sum(home_recv[...].reshape(32, 16, 128).astype(F32), axis=0)
     text_out[...] = jnp.concatenate([summed[4 * k : 4 * k + 4] for k in range(4)], axis=1).astype(BF16)
-    drain()
 
 
 def per_device(texts, frames, frame_mask, cotangent):
@@ -325,9 +320,11 @@
             jax.ShapeDtypeStruct((ROWS, D), BF16),
             jax.ShapeDtypeStruct((4, FR, D), BF16),
         ),
-        in_specs=[whole, remote, whole, remote],
+        in_specs=[remote] * 4,
         out_specs=(whole, whole),
         scratch_shapes=[
+            vmem((ROWS, D), BF16),
+            vmem((C_DEV, FR), jnp.int32),
             vmem((16, FR, D), BF16),
             vmem((16, 2048), F32),
             vmem((16, 128), BF16),
@@ -348,7 +345,7 @@
             vmem((2, GROUP, D), BF16),
             vmem((GROUP, D), BF16),
             vmem((GROUP, D), BF16),
-            dma((3,)), dma((3,)), dma((3,)), dma((NZ, 4)), dma((NZ,)), dma((4, NX)), dma((4, NX)),
+            dma((5,)), dma((3,)), dma((3,)), dma((NZ, 4)), dma((NZ,)), dma((4, NX)), dma((4, NX)),
             dma((4, 3)), dma((4, 3)), dma((4, 2, 4)), dma, dma((2,)), dma((2,)), dma, dma,
         ],
         compiler_params=pltpu.CompilerParams(

time: 44.4 us -> 43.8 us (0.986)
  Pallas kernels: 42.2 us -> 41.7 us
    pallas_call x1, Pallas kernels: 42.2 us -> 41.7 us  [per_device(): pl.pallas_call(kernel, out_shape=(jax.ShapeDtypeStruct((ROWS, D), BF16),...]
where the time goes in v5:
time: 43.8 us; the launch traced here: 43.7 us
  Pallas kernels  41.7 us (95%)
  local copies, waits for them, and re-layouts  1.27 us (3%)
  between operations  0.64 us (1%)
    pallas_call x1, Pallas kernels, per_device(): pl.pallas_call(kernel, out_shape=(jax.ShapeDtypeStruct((ROWS, D), BF16),...  41.7 us
    unnamed x2, local copies, waits for them, and re-layouts  1.27 us

profile of v5, /device:TPU:1, one launch (start us, length us, event | category | flops | bytes accessed | tf_op | source)
XLA Modules:
  0.0 43.7 jit_solution(11599877461194379322)
XLA Ops:
  0.6 41.7 %pooling_grads.1 = (bf16[4,512]{1,0:T(4,128)(2,1)S(1)}, bf16[4,48,512]{2,1,0:T(8,128)(2,1)S(1)}) custom-call(bf16[4,512]{1,0:T(4,128)(2,1)} %texts_hbm.1, bf16[16,48,512]{2,1,0:T(8,128)(2,1)} %frames_ref.1, s32[16,48]{1,0:T(8,128)} %mask_hbm.1, f32[16,2048]{1,0:T(8,128)} %bitcast.1), custom_call_target="tpu_custom_call" | custom-call | tf_op jit(solution)/shard_map/pooling_grads/pallas_call | solution.py:317
  42.4 0.6 %copy.8 = bf16[4,512]{1,0:T(4,128)(2,1)} copy(bf16[4,512]{1,0:T(4,128)(2,1)S(1)} %get-tuple-element.4) | data formatting | bytes 8192
  43.0 0.7 %copy.9 = bf16[4,48,512]{2,1,0:T(8,128)(2,1)} copy(bf16[4,48,512]{2,1,0:T(8,128)(2,1)S(1)} %get-tuple-element.5) | data formatting | bytes 393216

commit v6 on v5

--- a/solution.py
+++ b/solution.py
@@ -146,11 +146,10 @@
     pl.semaphore_wait(barrier, 8 * 5 - 1 + 3 + 1 + 1)
 
     mine = texts_in.at[z, x, rep]
-    for dz in FAR_Z:
-        for k, yy in enumerate(handlers):
-            if dz > 0 or k > 0:
-                to = device(x, (z + dz) % NZ, yy, core)
-                start(send(tile, mine, ag_send.at[dz, k], ag_recv.at[z], to))
+    for zz in range(NZ):
+        for k in (3, 1, 2, 0):
+            copy = send(tile, mine, ag_send.at[zz, k], ag_recv.at[z], device(x, zz, handlers[k], core))
+            start(copy, z != zz if k == 0 else None)
     pltpu.make_async_copy(tile, mine, ag_recv.at[z]).start()
 
     for load in loads:
@@ -194,14 +193,16 @@
     def spread(k):
         for zz in (2 * k, 2 * k + 1):
             arrived(texts_in.at[zz, x], ag_recv.at[zz])
-        line = texts_in.at[pl.ds(2 * k, 2), x]
-        for dx in FAR_X:
-            start(send(line, line, ag_x_send.at[k, dx], ag_x_recv.at[k, x], device((x + dx) % NX, z, y, core)))
+            line = texts_in.at[zz, x]
+            for dx in FAR_X:
+                to = device((x + dx) % NX, z, y, core)
+                start(send(line, line, ag_x_send.at[zz, dx], ag_x_recv.at[zz, x], to))
 
     def work(k):
         for dx in FAR_X:
             xx = (x + dx) % NX
-            arrived(texts_in.at[pl.ds(2 * k, 2), xx], ag_x_recv.at[k, xx])
+            for zz in (2 * k, 2 * k + 1):
+                arrived(texts_in.at[zz, xx], ag_x_recv.at[zz, xx])
         columns = slice(CHUNK * k, CHUNK * k + CHUNK)
         tiles = texts_in[2 * k : 2 * k + 2].reshape(32, 16, 128).astype(F32)
         for i, block in enumerate(tiles_to_rows(tiles)):
@@ -345,7 +346,7 @@
             vmem((2, GROUP, D), BF16),
             vmem((GROUP, D), BF16),
             vmem((GROUP, D), BF16),
-            dma((5,)), dma((3,)), dma((3,)), dma((NZ, 4)), dma((NZ,)), dma((4, NX)), dma((4, NX)),
+            dma((5,)), dma((3,)), dma((3,)), dma((NZ, 4)), dma((NZ,)), dma((NZ, NX)), dma((NZ, NX)),
             dma((4, 3)), dma((4, 3)), dma((4, 2, 4)), dma, dma((2,)), dma((2,)), dma, dma,
         ],
         compiler_params=pltpu.CompilerParams(

time: 43.8 us -> 43.6 us (level); the launches traced: 43.7 us -> 42.9 us
  Pallas kernels: 41.7 us -> 41 us
    pallas_call x1, Pallas kernels: 41.7 us -> 41 us  [per_device(): pl.pallas_call(kernel, out_shape=(jax.ShapeDtypeStruct((ROWS, D), BF16),...]
where the time goes in v6:
time: 43.6 us; the launch traced here: 42.9 us
  Pallas kernels  41 us (94%)
  local copies, waits for them, and re-layouts  1.27 us (3%)
  between operations  0.64 us (1%)
    pallas_call x1, Pallas kernels, per_device(): pl.pallas_call(kernel, out_shape=(jax.ShapeDtypeStruct((ROWS, D), BF16),...  41 us
    unnamed x2, local copies, waits for them, and re-layouts  1.27 us

profile of v6, /device:TPU:1, one launch (start us, length us, event | category | flops | bytes accessed | tf_op | source)
XLA Modules:
  0.0 42.9 jit_solution(2362208308655421769)
XLA Ops:
  0.6 41.0 %pooling_grads.1 = (bf16[4,512]{1,0:T(4,128)(2,1)S(1)}, bf16[4,48,512]{2,1,0:T(8,128)(2,1)S(1)}) custom-call(bf16[4,512]{1,0:T(4,128)(2,1)} %texts_hbm.1, bf16[16,48,512]{2,1,0:T(8,128)(2,1)} %frames_ref.1, s32[16,48]{1,0:T(8,128)} %mask_hbm.1, f32[16,2048]{1,0:T(8,128)} %bitcast.1), custom_call_target="tpu_custom_call" | custom-call | tf_op jit(solution)/shard_map/pooling_grads/pallas_call | solution.py:318
  41.6 0.6 %copy.8 = bf16[4,512]{1,0:T(4,128)(2,1)} copy(bf16[4,512]{1,0:T(4,128)(2,1)S(1)} %get-tuple-element.4) | data formatting | bytes 8192
  42.2 0.7 %copy.9 = bf16[4,48,512]{2,1,0:T(8,128)(2,1)} copy(bf16[4,48,512]{2,1,0:T(8,128)(2,1)S(1)} %get-tuple-element.5) | data formatting | bytes 393216
